TPU v7x, 128 devices: a whole 4x4x4 slice. The times are simulated.
128 devices in a mesh: lon: 8 (over y, core), lat: 16 (over x, z).
Axes of the slice: x: 4, y: 4, z: 4, core: 2. Of those that a mesh axis runs over, the one named last changes fastest.
Arguments:
- grid: bfloat16 [12, 2, 2, 1024, 4096], P(None, None, None, 'lat', 'lon'), may hold values from -6 to 6
- legendre: bfloat16 [8, 128, 1024, 2, 512], P('lon', None, 'lat'), may hold values from -0.25 to 0.25
Outputs:
- spectral: float32 [8, 128, 8, 2, 2, 2, 512], P('lon', 'lat')
All inputs are finite; a program needn't handle non-finite values.
Results may differ from a plain program's by a relative error of at most 0.0029.
Values sent between devices are 32-bit elements; how exact they have to be, the bound alone decides.
A program may use at most 128 MiB of HBM per device.

v0:
```python
import math

import jax
import jax.numpy as jnp
from jax import lax
from jax.sharding import PartitionSpec as P

NLON = 4096
WAVES = 1024


adiabatic_exponent = 0.286


def tendency_fields(numeric_buffer_grid):
    eastward_flow_speed, poleward_flow_speed, local_spin_field, flow_spreading_rate = (
        numeric_buffer_grid[0],
        numeric_buffer_grid[1],
        numeric_buffer_grid[2],
        numeric_buffer_grid[3],
    )
    kinetic_warmth_field, water_vapour_mixing = (numeric_buffer_grid[4], numeric_buffer_grid[5])
    warmth_eastward_slope, warmth_poleward_slope = (numeric_buffer_grid[6], numeric_buffer_grid[7])
    vapour_eastward_slope, vapour_poleward_slope = (numeric_buffer_grid[8], numeric_buffer_grid[9])
    ground_load_eastward_slope, ground_load_poleward_slope = (
        numeric_buffer_grid[10],
        numeric_buffer_grid[11],
    )
    return jnp.stack(
        [
            local_spin_field * poleward_flow_speed
            - kinetic_warmth_field * ground_load_eastward_slope,
            -local_spin_field * eastward_flow_speed
            - kinetic_warmth_field * ground_load_poleward_slope,
            eastward_flow_speed * poleward_flow_speed,
            -(
                eastward_flow_speed * warmth_eastward_slope
                + poleward_flow_speed * warmth_poleward_slope
            )
            + adiabatic_exponent * kinetic_warmth_field * flow_spreading_rate,
            -(
                eastward_flow_speed * vapour_eastward_slope
                + poleward_flow_speed * vapour_poleward_slope
            )
            - water_vapour_mixing * flow_spreading_rate,
            eastward_flow_speed * kinetic_warmth_field,
            poleward_flow_speed * kinetic_warmth_field,
            poleward_flow_speed * water_vapour_mixing,
        ],
        0,
    )


def phase_rows(lon_first, lon_number, devices, per_device):
    longitude = lon_first + lax.iota(jnp.int32, lon_number)
    owners = lax.iota(jnp.int32, devices)
    column = lax.iota(jnp.int32, per_device)
    wavenumber = owners[:, None] + devices * column[None, :]
    product = wavenumber[:, :, None] * longitude[None, None, :] % NLON
    angles = product.astype(jnp.float32) * (2.0 * math.pi / NLON)
    factor = 1.0 / math.sqrt(NLON)
    return jnp.stack([jnp.cos(angles) * factor, -jnp.sin(angles) * factor], 1)


def spectra_level(grid, legendre):
    tendencies = tendency_fields(grid.astype(jnp.float32))
    tend_shape = tendencies.shape
    lon_local = tend_shape[4]
    row_count = tend_shape[0] * tend_shape[1] * tend_shape[2] * tend_shape[3]
    flattened = tendencies.reshape(row_count, lon_local)
    devices = lax.axis_size("lon")
    lon_rank = lax.axis_index("lon")
    per_device = legendre.shape[1]
    phases = phase_rows(lon_rank * lon_local, lon_local, devices, per_device)
    section = phases
    received = lax.psum_scatter(
        lax.dot_general(
            section,
            flattened,
            (((3,), (1,)), ((), ())),
            precision=lax.Precision.HIGHEST,
            preferred_element_type=jnp.float32,
        ),
        "lon",
        scatter_dimension=0,
        tiled=True,
    )
    spectra = received.reshape(2, per_device, row_count)
    shaped = spectra.reshape(2, per_device, tend_shape[0], tend_shape[1], 2, tend_shape[3])
    northern = shaped[:, :, :, :, 0]
    southern = shaped[:, :, :, :, 1]
    folded = jnp.stack([northern + southern, northern - southern], 0).astype(jnp.bfloat16)
    weights = legendre[0]
    lat_count = lax.axis_size("lat")
    own_rows = per_device // lat_count
    half_degrees = weights.shape[-1]
    section = weights
    result = lax.psum_scatter(
        jnp.einsum("ecsklj,sjeh->sklceh", folded, section, preferred_element_type=jnp.float32),
        "lat",
        scatter_dimension=0,
        tiled=True,
    )
    column = lax.axis_index("lat") * own_rows + lax.iota(jnp.int32, own_rows)
    wavenumber = lon_rank + devices * column
    degree = (
        2 * lax.iota(jnp.int32, half_degrees)[None, None, :] + lax.iota(jnp.int32, 2)[None, :, None]
    )
    inside = wavenumber[:, None, None] + degree < WAVES
    result = jnp.where(inside[:, None, None, None, :, :], result, jnp.zeros((), jnp.float32))
    return result[None]


def local(grid, legendre):
    return spectra_level(grid, legendre)


def solution(mesh):
    in_specs = (P(None, None, None, "lat", "lon"), P("lon", None, "lat", None, None))
    out_specs = P("lon", "lat", None, None, None, None, None)
    return jax.shard_map(local, mesh=mesh, in_specs=in_specs, out_specs=out_specs, check_vma=False)
```

profile of v0, /device:TPU:0, one launch (start us, length us, event | category | flops | bytes accessed | tf_op | source)
XLA Modules:
  0.0 295.1 jit_solution(557117933657497165)
XLA Ops:
  6.5 0.0 reduce-scatter.3.cloned.1.call-start
  6.5 2.7 convert_element_type.19
  9.3 1.0 fusion.28
  10.3 1.0 fusion.26
  11.3 0.9 multiply_dynamic-update-slice_fusion.3
  12.2 1.1 fusion.24
  13.3 1.2 fusion.20
  14.5 0.9 multiply_dynamic-update-slice_fusion.2
  15.4 0.9 multiply_dynamic-update-slice_fusion.1
  16.3 0.9 multiply_dynamic-update-slice_fusion
  17.1 8.4 %cosine_multiply_fusion = (f32[8,1,128,512]{3,2,1,0:T(8,128)S(1)}, f32[8,1,128,512]{3,2,1,0:T(8,128)S(1)}) fusion(s32[512]{0:T(512)S(1)} %iota_add_fusion.2, s32[8,128]{1,0:T(8,128)S(1)} %iota_add_fusion), kind=kLoop, calls=%fused_computation.21 | loop fusion | flops 8912896 | bytes 4200448 | tf_op jit(solution)/shard_map/mul | solution.py:62
  25.5 31.0 %fusion.5 = f32[8,2,128,2048]{3,2,1,0:T(8,128)} fusion(f32[2048,512,1,1]{1,0,3,2:T(8,128)} %bitcast.2, f32[8,1,128,512]{3,2,1,0:T(8,128)S(1)} %get-tuple-element.10, f32[8,1,128,512]{3,2,1,0:T(8,128)S(1)} %get-tuple-element.9), kind=kOutput, calls=%fused_computation.3 | convolution fusion | flops 25770852352 | bytes 25165824 | tf_op jit(solution)/shard_map/dot_general | solution.py:77
  56.5 0.0 reduce-scatter.3.cloned.1.call-update
  56.5 0.0 reduce-scatter.5.cloned.1.call-start
  56.6 94.3 %reduce-scatter.3.cloned.1.call-done = f32[1,2,128,2048]{3,2,1,0:T(8,128)} async-done(((f32[8,2,128,2048]{3,2,1,0:T(8,128)}), f32[1,2,128,2048]{3,2,1,0:T(8,128)}) %reduce-scatter.3.cloned.1.call-update) | async-done | bytes 2097168 | tf_op jit(solution)/shard_map/reduce_scatter | solution.py:76
  150.9 1.9 copy.8
  152.8 1.2 fusion.31
  154.0 3.1 %copy.18 = f32[2,128,8,2,1,64]{5,2,3,0,1,4:T(8,128)S(1)} copy(f32[2,128,8,2,1,64]{1,5,4,3,2,0:T(8,128)} %get-tuple-element.8) | data formatting | bytes 2097152
  157.0 2.8 copy.19
  159.9 2.1 fusion.15
  162.0 12.6 %fusion.2 = f32[128,8,2,2,2,512]{5,1,2,3,4,0:T(8,128)} fusion(bf16[128,64,2,512,1,1]{3,2,1,0,5,4:T(2,128)(2,1)} %bitcast.20, bf16[1,2,128,8,2,64]{5,3,4,1,0,2:T(8,128)(2,1)S(1)} %get-tuple-element.6, bf16[1,2,128,8,2,64]{5,3,4,1,0,2:T(8,128)(2,1)S(1)} %get-tuple-element.5), kind=kOutput, calls=%fused_computation.2 | convolution fusion | flops 537395200 | bytes 34603008 | tf_op jit(solution)/shard_map/ecsklj,sjeh->sklceh/dot_general | solution.py:99
  174.5 0.0 reduce-scatter.5.cloned.1.call-update
  174.6 0.1 add_compare_fusion
  174.7 110.4 %reduce-scatter.5.cloned.1.call-done = f32[8,8,2,2,2,512]{5,1,2,3,4,0:T(8,128)} async-done(((f32[128,8,2,2,2,512]{5,1,2,3,4,0:T(8,128)}), f32[8,8,2,2,2,512]{5,1,2,3,4,0:T(8,128)}) %reduce-scatter.5.cloned.1.call-update) | async-done | bytes 1048592 | tf_op jit(solution)/shard_map/reduce_scatter | solution.py:98
  285.1 1.3 select_bitcast_fusion
  286.4 1.8 copy.13
  (6 shorter events, 0.0 us)
Async XLA Ops:
  6.5 144.4 %reduce-scatter.3.cloned.1.call-start = ((), (), s32[]{:S(2)}) async-start(), calls=%async_computation.2 | async-start | bytes 18874368 | tf_op jit(solution)/shard_map/reduce_scatter | solution.py:76
  56.5 228.5 %reduce-scatter.5.cloned.1.call-start = ((), (), s32[]{:S(2)}) async-start(), calls=%async_computation.3 | async-start | bytes 17825792 | tf_op jit(solution)/shard_map/reduce_scatter | solution.py:98
Sparse Core Ops, SparseCore 0:
  56.7 94.1 reduce-scatter.2
  174.7 110.3 reduce-scatter.4
where the time goes:
time: 296 us; the launch traced here: 295 us
  waiting for transfers between devices  205 us (69%)
  matrix products  43.6 us (15%)
  other arithmetic  22.5 us (8%)
  between operations  13.5 us (5%)
  local copies, waits for them, and re-layouts  10.7 us (4%)
    reduce_scatter x1, waiting for transfers between devices, spectra_level(): lax.psum_scatter(jnp.einsum('ecsklj,sjeh->sklceh', folded, section, prefe...  110 us
    reduce_scatter x1, waiting for transfers between devices, spectra_level(): lax.psum_scatter(lax.dot_general(section, flattened, (((3,), (1,)), ((),...  94.3 us
    dot_general x1, matrix products, spectra_level(): lax.dot_general(section, flattened, (((3,), (1,)), ((), ())), precision=l...  31 us
    dot_general x1, matrix products, spectra_level(): jnp.einsum('ecsklj,sjeh->sklceh', folded, section, preferred_element_type...  12.6 us
    mul x1, other arithmetic, phase_rows(): return jnp.stack([jnp.cos(angles) * factor, -jnp.sin(angles) * factor], 1)  8.36 us
    unnamed x7, other arithmetic  6.98 us
  transfers between devices with their start and end apart: 2, of which 2 were waited for; matrix products, arithmetic and copies ran while one was open for 0% of the time, Pallas kernels for 0%

commit v1 on v0

v1 whole, which is shorter than its diff:
```python
import jax
import jax.numpy as jnp
import numpy as np
from jax import lax
from jax.experimental import pallas as pl
from jax.experimental.pallas import tpu as pltpu
from jax.sharding import PartitionSpec as P

NLON = 4096
WAVES = 1024
LON_DEV = 8
LAT_DEV = 16
LON_LOCAL = NLON // LON_DEV
ROWS = 2048
CHUNKS = 8
UNITS = (4, 3, 2, 1)
OFFSETS = (0, 4, 7, 9)
TOTAL = 10
ADIABATIC = 0.286
ROOT_HALF = 0.5**0.5


def phase_table():
    i, core, y, k = np.meshgrid(
        np.arange(CHUNKS), np.arange(2), np.arange(4), np.arange(LAT_DEV), indexing="ij"
    )
    m = 2 * y + core + LON_DEV * (CHUNKS * k + i)
    turns = m[..., None] * np.arange(LON_LOCAL) % NLON
    angles = turns * (2.0 * np.pi / NLON)
    table = np.stack([np.cos(angles), -np.sin(angles)], 3) / np.sqrt(NLON)
    return table.reshape(CHUNKS, 8, 2, LAT_DEV, LON_LOCAL).astype(np.float32)


def eighth_cos(n):
    n = lax.rem(n, 8)
    value = jnp.float32(1.0)
    for at, root in ((1, ROOT_HALF), (2, 0.0), (3, -ROOT_HALF), (4, -1.0), (5, -ROOT_HALF), (6, 0.0), (7, ROOT_HALF)):
        value = jnp.where(n == at, jnp.float32(root), value)
    return value


def tendencies(f):
    u, v, zeta, div, temp, hum, temp_x, temp_y, hum_x, hum_y, press_x, press_y = f
    return (
        zeta * v - temp * press_x,
        -zeta * u - temp * press_y,
        u * v,
        -(u * temp_x + v * temp_y) + ADIABATIC * temp * div,
        -(u * hum_x + v * hum_y) - hum * div,
        u * temp,
        v * temp,
        v * hum,
    )


def split_bf16(a):
    high = a.astype(jnp.bfloat16)
    return high, (a - high.astype(jnp.float32)).astype(jnp.bfloat16)


NT = (((1,), (1,)), ((), ()))


def kernel(
    grid_ref, table_ref, leg_ref, out_ref,
    t_hi, t_lo, mix, table, phases, part, paired, y1_in, y2_in, fold, leg, spec, z1_in, z2_in, x_in,
    table_sem, leg_sem, core_s, core_r, y1_s, y1_r, y2_s, y2_r, z1_s, z1_r, z2_s, z2_r, x_s, x_r,
):
    r = lax.axis_index("lon")
    k = lax.axis_index("lat")
    y, core = r // 2, lax.rem(r, 2)
    x, z = k // 4, lax.rem(k, 4)
    y_up, y_down = lax.rem(y + 1, 4), lax.rem(y + 3, 4)
    z_up, z_down = lax.rem(z + 1, 4), lax.rem(z + 3, 4)
    y_far, z_far = lax.rem(y + 2, 4), lax.rem(z + 2, 4)

    def lon_dev(yy, cc):
        return {"lon": yy * 2 + cc}

    def lat_dev(xx, zz):
        return {"lat": xx * 4 + zz}

    def send(src, dst, s, q, dev):
        return pltpu.make_async_remote_copy(
            src_ref=src, dst_ref=dst, send_sem=s, recv_sem=q, device_id=dev, device_id_type=pl.DeviceIdType.MESH
        )

    def table_copy(t):
        return pltpu.make_async_copy(table_ref.at[t], table.at[t], table_sem.at[t])

    def leg_copy(t):
        slot = lax.rem(t, 2)
        return pltpu.make_async_copy(leg_ref.at[:, t], leg.at[slot], leg_sem.at[slot])

    def core_copy(t):
        return send(
            part.at[lax.rem(t, 2), 1 - core], paired.at[t], core_s.at[t], core_r.at[t], lon_dev(y, 1 - core)
        )

    def y1_copies(t):
        return (
            send(paired.at[t, y_far, 0], y1_in.at[t, 0], y1_s.at[t, 0], y1_r.at[t, 0], lon_dev(y_up, core)),
            send(paired.at[t, y_far, 1], y1_in.at[t, 1], y1_s.at[t, 1], y1_r.at[t, 1], lon_dev(y_down, core)),
        )

    def y2_copies(t):
        return (
            send(paired.at[t, y_up], y2_in.at[t, 0], y2_s.at[t, 0], y2_r.at[t, 0], lon_dev(y_up, core)),
            send(paired.at[t, y_down], y2_in.at[t, 1], y2_s.at[t, 1], y2_r.at[t, 1], lon_dev(y_down, core)),
        )

    half = TOTAL // 2

    def z1_copies(t):
        return (
            send(spec.at[t, z_far, 0:half], z1_in.at[t, 0], z1_s.at[t, 0], z1_r.at[t, 0], lat_dev(x, z_up)),
            send(spec.at[t, z_far, half:TOTAL], z1_in.at[t, 1], z1_s.at[t, 1], z1_r.at[t, 1], lat_dev(x, z_down)),
        )

    def z2_copies(t):
        return (
            send(spec.at[t, z_up], z2_in.at[t, 0], z2_s.at[t, 0], z2_r.at[t, 0], lat_dev(x, z_up)),
            send(spec.at[t, z_down], z2_in.at[t, 1], z2_s.at[t, 1], z2_r.at[t, 1], lat_dev(x, z_down)),
        )

    def x_copy(t, source, to):
        n, first = UNITS[to], OFFSETS[to]
        return send(
            spec.at[t, z, first : first + n], x_in.at[t, source, 0:n], x_s.at[t, to], x_r.at[t, source], lat_dev(to, z)
        )

    for t in range(CHUNKS):
        table_copy(t).start()
    for t in range(2):
        leg_copy(t).start()

    barrier = pltpu.get_barrier_semaphore()
    for dev in (lon_dev(y, 1 - core), lon_dev(y_up, core), lon_dev(y_down, core), lat_dev(x, z_up), lat_dev(x, z_down)):
        pl.semaphore_signal(barrier, inc=1, device_id=dev, device_id_type=pl.DeviceIdType.MESH)
    for step in range(1, 4):
        dev = lat_dev(lax.rem(x + step, 4), z)
        pl.semaphore_signal(barrier, inc=1, device_id=dev, device_id_type=pl.DeviceIdType.MESH)

    def fields(step, carry):
        level, block = step // 4, lax.rem(step, 4)
        first = pl.multiple_of(block * 16, 16)
        for lane in range(4):
            lanes = pl.ds(lane * 128, 128)
            north, south = (
                tendencies([grid_ref[f, level, h, pl.ds(first, 16), lanes].astype(jnp.float32) for f in range(12)])
                for h in range(2)
            )
            for t in range(8):
                mix[lane * 8 + t, pl.ds(0, 16, stride=2), :] = north[t] + south[t]
                mix[lane * 8 + t, pl.ds(1, 16, stride=2), :] = north[t] - south[t]
            for t in range(8):
                high, low = split_bf16(mix[lane * 8 + t])
                at = pl.multiple_of((2 * t + level) * 128 + block * 32, 32)
                t_hi[pl.ds(at, 32), lanes] = high
                t_lo[pl.ds(at, 32), lanes] = low
        return carry

    lax.fori_loop(0, 8, fields, 0)

    pl.semaphore_wait(barrier, 8)

    def analyse(t):
        slot = lax.rem(t, 2)
        table_copy(t).wait()

        def rotate(block, carry):
            q = 2 * lax.rem(block, 4) + block // 4
            c, s = eighth_cos(r * q), eighth_cos(r * q + 6)
            real, imag = table[t, block, 0], table[t, block, 1]
            for part_index, value in enumerate((real * c + imag * s, imag * c - real * s)):
                high, low = split_bf16(value)
                at = pl.multiple_of(block * 32 + part_index * 16, 16)
                phases[pl.ds(at, 16), :] = high
                phases[pl.ds(at + 256, 16), :] = low
            return carry

        lax.fori_loop(0, 8, rotate, 0)

        @pl.when(t >= 2)
        def _():
            core_copy(t - 2).wait_send()

        def columns(n, carry):
            rows = pl.ds(pl.multiple_of(n * 256, 256), 256)
            both = lax.dot_general(phases[...], t_hi[rows, :], NT, preferred_element_type=jnp.float32)
            rest = lax.dot_general(phases[0:256, :], t_lo[rows, :], NT, preferred_element_type=jnp.float32)
            value = both[0:256] + (both[256:512] + rest)
            part[slot, :, :, :, :, rows] = value.reshape(2, 4, 2, 16, 256)
            return carry

        lax.fori_loop(0, 8, columns, 0)
        core_copy(t).start()

    def pair_sum(t):
        slot = lax.rem(t, 2)
        core_copy(t).wait_recv()

        def add(n, carry):
            yy = lax.rem(y_far + n, 4)
            paired[t, yy] = paired[t, yy] + part[slot, core, yy]
            return carry

        lax.fori_loop(0, 4, add, 0)
        for copy in y1_copies(t):
            copy.start()

    def y_forward(t):
        for copy in y1_copies(t):
            copy.wait_recv()
        paired[t, y_up, 0] = paired[t, y_up, 0] + y1_in[t, 0]
        paired[t, y_down, 1] = paired[t, y_down, 1] + y1_in[t, 1]
        for copy in y2_copies(t):
            copy.start()

    def project(t):
        slot = lax.rem(t, 2)
        for copy in y2_copies(t):
            copy.wait_recv()
        for c in range(2):
            for tl in range(16):
                lanes = pl.ds(tl * 128, 128)
                value = paired[t, y, c, :, lanes] + (y2_in[t, 0, c, :, lanes] + y2_in[t, 1, c, :, lanes])
                fold[pl.ds(tl * 2 + c, 16, stride=32), :] = value
        leg_copy(t).wait()
        even = lax.rem(lax.broadcasted_iota(jnp.int32, (32, 128), 1), 2) == 0
        for owner in range(LAT_DEV):
            ox, oz = owner // 4, owner % 4
            rows = fold[owner * 32 : owner * 32 + 32, :]
            zero = jnp.zeros_like(rows)
            left = jnp.concatenate([jnp.where(even, rows, zero), jnp.where(even, zero, rows)], 0).astype(jnp.bfloat16)
            n = UNITS[ox]
            right = leg[slot, owner, :, :, 0 : 128 * n].reshape(128, 128 * n)
            value = jnp.dot(left, right, preferred_element_type=jnp.float32)
            for unit in range(n):
                spec[t, oz, OFFSETS[ox] + unit] = value[:, unit * 128 : unit * 128 + 128]
        for copy in z1_copies(t):
            copy.start()

        @pl.when(t + 2 < CHUNKS)
        def _():
            leg_copy(t + 2).start()

    def z_forward(t):
        for copy in z1_copies(t):
            copy.wait_recv()
        spec[t, z_up, 0:half] = spec[t, z_up, 0:half] + z1_in[t, 0]
        spec[t, z_down, half:TOTAL] = spec[t, z_down, half:TOTAL] + z1_in[t, 1]
        for copy in z2_copies(t):
            copy.start()

    def x_start(t):
        for copy in z2_copies(t):
            copy.wait_recv()
        spec[t, z] = spec[t, z] + (z2_in[t, 0] + z2_in[t, 1])
        for to in range(4):

            @pl.when(x != to)
            def _():
                x_copy(t, x, to).start()

    def finish(t):
        order = r + LON_DEV * (CHUNKS * k + t)
        for mine in range(4):

            @pl.when(x == mine)
            def _():
                n, first = UNITS[mine], OFFSETS[mine]
                others = [source for source in range(4) if source != mine]
                for source in others:
                    x_copy(t, source, mine).wait_recv()
                lane = lax.broadcasted_iota(jnp.int32, (32, 128), 1)
                for unit in range(4):
                    for e in range(2):
                        lanes = pl.ds(e * 512 + unit * 128, 128)
                        if unit >= n:
                            out_ref[t, :, lanes] = jnp.zeros((32, 128), jnp.float32)
                            continue
                        rows = pl.ds(e * 32, 32)
                        value = spec[t, z, first + unit, rows, :]
                        for source in others:
                            value = value + x_in[t, source, unit, rows, :]
                        inside = order + 2 * (lane + unit * 128) + e < WAVES
                        out_ref[t, :, lanes] = jnp.where(inside, value, jnp.zeros_like(value))

    def stage(run, t):
        @pl.when((t >= 0) & (t < CHUNKS))
        def _():
            run(t)

    def steps(step, carry):
        t = step - 2
        stage(y_forward, t)
        stage(project, t - 1)
        stage(x_start, t - 2)
        stage(analyse, t + 2)
        stage(z_forward, t - 1)
        stage(pair_sum, t + 2)
        stage(finish, t - 3)
        return carry

    lax.fori_loop(0, CHUNKS + 5, steps, 0)

    def drain(t, carry):
        @pl.when(t >= CHUNKS - 2)
        def _():
            core_copy(t).wait_send()

        for copy in (*y1_copies(t), *y2_copies(t), *z1_copies(t), *z2_copies(t)):
            copy.wait_send()
        for to in range(4):

            @pl.when(x != to)
            def _():
                x_copy(t, x, to).wait_send()

        return carry

    lax.fori_loop(0, CHUNKS, drain, 0)


def local(grid, legendre):
    table = jnp.asarray(phase_table())
    f32, bf16 = jnp.float32, jnp.bfloat16
    dma = pltpu.SemaphoreType.DMA
    result = pl.pallas_call(
        kernel,
        out_shape=jax.ShapeDtypeStruct((CHUNKS, 32, WAVES), f32),
        in_specs=[
            pl.BlockSpec(memory_space=pltpu.VMEM),
            pl.BlockSpec(memory_space=pl.ANY),
            pl.BlockSpec(memory_space=pl.ANY),
        ],
        out_specs=pl.BlockSpec(memory_space=pltpu.VMEM),
        scratch_shapes=[
            pltpu.VMEM((ROWS, LON_LOCAL), bf16),
            pltpu.VMEM((ROWS, LON_LOCAL), bf16),
            pltpu.VMEM((32, 32, 128), f32),
            pltpu.VMEM((CHUNKS, 8, 2, 16, LON_LOCAL), f32),
            pltpu.VMEM((512, LON_LOCAL), bf16),
            pltpu.VMEM((2, 2, 4, 2, 16, ROWS), f32),
            pltpu.VMEM((CHUNKS, 4, 2, 16, ROWS), f32),
            pltpu.VMEM((CHUNKS, 2, 16, ROWS), f32),
            pltpu.VMEM((CHUNKS, 2, 2, 16, ROWS), f32),
            pltpu.VMEM((512, 128), f32),
            pltpu.VMEM((2, 16, 64, 2, 512), bf16),
            pltpu.VMEM((CHUNKS, 4, TOTAL, 64, 128), f32),
            pltpu.VMEM((CHUNKS, 2, TOTAL // 2, 64, 128), f32),
            pltpu.VMEM((CHUNKS, 2, TOTAL, 64, 128), f32),
            pltpu.VMEM((CHUNKS, 4, 4, 64, 128), f32),
            dma((CHUNKS,)),
            dma((2,)),
            dma((CHUNKS,)),
            dma((CHUNKS,)),
            *[dma((CHUNKS, 2)) for _ in range(8)],
            dma((CHUNKS, 4)),
            dma((CHUNKS, 4)),
        ],
        compiler_params=pltpu.CompilerParams(
            collective_id=0, has_side_effects=True, vmem_limit_bytes=62 * 2**20
        ),
        name="spectral",
    )(grid, table, legendre.reshape(LAT_DEV, CHUNKS, 64, 2, 512))
    return result.reshape(1, CHUNKS, 8, 2, 2, 2, 512)


def solution(mesh):
    in_specs = (P(None, None, None, "lat", "lon"), P("lon", None, "lat", None, None))
    out_specs = P("lon", "lat", None, None, None, None, None)
    return jax.shard_map(local, mesh=mesh, in_specs=in_specs, out_specs=out_specs, check_vma=False)
```

time: 296 us -> 139 us (0.47)
  waiting for transfers between devices: 205 us -> 0 us
  Pallas kernels: 0 us -> 136 us
  matrix products: 43.6 us -> 0 us
  other arithmetic: 22.5 us -> 0 us
  between operations: 13.5 us -> 0.01 us
  local copies, waits for them, and re-layouts: 10.7 us -> 3.08 us
    reduce_scatter x2 -> x0, waiting for transfers between devices: 205 us -> none  [the longest x1 110 us: spectra_level(): lax.psum_scatter(jnp.einsum('ecsklj,sjeh->sklceh', folded, section, prefe...]
    pallas_call x0 -> x1, Pallas kernels: none -> 136 us  [local(): pl.pallas_call(kernel, out_shape=jax.ShapeDtypeStruct((CHUNKS, 32, WAVES)...]
    dot_general x2 -> x0, matrix products: 43.6 us -> none  [the longest x1 31 us: spectra_level(): lax.dot_general(section, flattened, (((3,), (1,)), ((), ())), precision=l...]
    mul x3 -> x0, other arithmetic: 8.37 us -> none  [the longest x1 8.36 us: phase_rows(): return jnp.stack([jnp.cos(angles) * factor, -jnp.sin(angles) * factor], 1)]
    unnamed x7 -> x0, other arithmetic: 6.98 us -> none
    unnamed x2 -> x0, local copies, waits for them, and re-layouts: 5.88 us -> none
    reshape x0 -> x1, local copies, waits for them, and re-layouts: none -> 3.08 us  [local(): return result.reshape(1, CHUNKS, 8, 2, 2, 2, 512)]
  transfers between devices with their start and end apart: 2 -> 0, of which waited for: 2 -> 0; matrix products, arithmetic and copies ran while one was open for 0% -> 0% of each run, Pallas kernels for 0% -> 0%
where the time goes in v1:
time: 139 us
  Pallas kernels  136 us (98%)
  local copies, waits for them, and re-layouts  3.08 us (2%)
    pallas_call x1, Pallas kernels, local(): pl.pallas_call(kernel, out_shape=jax.ShapeDtypeStruct((CHUNKS, 32, WAVES)...  136 us
    reshape x1, local copies, waits for them, and re-layouts, local(): return result.reshape(1, CHUNKS, 8, 2, 2, 2, 512)  3.08 us

profile of v1, /device:TPU:0, one launch (start us, length us, event | category | flops | bytes accessed | tf_op | source)
XLA Modules:
  0.0 139.1 jit_solution(2967954031868795928)
XLA Ops:
  0.0 136.0 %spectral.1 = f32[8,32,1024]{2,1,0:T(8,128)} custom-call(bf16[12,2,2,64,512]{4,3,2,1,0:T(8,128)(2,1)} %grid_ref.1, f32[8,8,2,16,512]{4,3,2,1,0:T(8,128)} %constant.2.clone.table_ref, bf16[16,8,64,2,512]{4,3,2,1,0:T(2,128)(2,1)} %bitcast.1), custom_call_target="tpu_custom_call" | custom-call | tf_op jit(solution)/shard_map/spectral/pallas_call | solution.py:330
  136.0 3.1 %reshape.7 = f32[1,8,8,2,2,2,512]{6,5,4,3,2,1,0:T(2,128)} reshape(f32[8,32,1024]{2,1,0:T(8,128)} %spectral.1) | data formatting | bytes 2097152 | tf_op jit(solution)/shard_map/reshape | solution.py:368

commit v2 on v1

--- a/solution.py
+++ b/solution.py
@@ -14,8 +14,9 @@
 ROWS = 2048
 CHUNKS = 8
 UNITS = (4, 3, 2, 1)
-OFFSETS = (0, 4, 7, 9)
-TOTAL = 10
+Z_UNITS = (3, 2, 1, 0)
+Z_OFFSETS = (0, 3, 5, 6)
+Z_TOTAL = 6
 ADIABATIC = 0.286
 ROOT_HALF = 0.5**0.5
 
@@ -63,8 +64,10 @@
 
 def kernel(
     grid_ref, table_ref, leg_ref, out_ref,
-    t_hi, t_lo, mix, table, phases, part, paired, y1_in, y2_in, fold, leg, spec, z1_in, z2_in, x_in,
-    table_sem, leg_sem, core_s, core_r, y1_s, y1_r, y2_s, y2_r, z1_s, z1_r, z2_s, z2_r, x_s, x_r,
+    t_hi, t_lo, mix, table, phases, part, paired, y1_in, y2_in, fold, leg,
+    spec_z, spec_x, z1_in, z2_in, zx_in, x1_in, x2_in, xz_in,
+    table_sem, leg_sem, core_s, core_r, y1_s, y1_r, y2_s, y2_r,
+    z1_s, z1_r, z2_s, z2_r, x1_s, x1_r, x2_s, x2_r, zx_s, zx_r, xz_s, xz_r,
 ):
     r = lax.axis_index("lon")
     k = lax.axis_index("lat")
@@ -72,7 +75,8 @@
     x, z = k // 4, lax.rem(k, 4)
     y_up, y_down = lax.rem(y + 1, 4), lax.rem(y + 3, 4)
     z_up, z_down = lax.rem(z + 1, 4), lax.rem(z + 3, 4)
-    y_far, z_far = lax.rem(y + 2, 4), lax.rem(z + 2, 4)
+    x_up, x_down = lax.rem(x + 1, 4), lax.rem(x + 3, 4)
+    x_far, y_far, z_far = lax.rem(x + 2, 4), lax.rem(y + 2, 4), lax.rem(z + 2, 4)
 
     def lon_dev(yy, cc):
         return {"lon": yy * 2 + cc}
@@ -109,25 +113,46 @@
             send(paired.at[t, y_down], y2_in.at[t, 1], y2_s.at[t, 1], y2_r.at[t, 1], lon_dev(y_down, core)),
         )
 
-    half = TOTAL // 2
+    z_half = Z_TOTAL // 2
 
     def z1_copies(t):
         return (
-            send(spec.at[t, z_far, 0:half], z1_in.at[t, 0], z1_s.at[t, 0], z1_r.at[t, 0], lat_dev(x, z_up)),
-            send(spec.at[t, z_far, half:TOTAL], z1_in.at[t, 1], z1_s.at[t, 1], z1_r.at[t, 1], lat_dev(x, z_down)),
+            send(spec_z.at[t, z_far, 0:z_half], z1_in.at[t, 0], z1_s.at[t, 0], z1_r.at[t, 0], lat_dev(x, z_up)),
+            send(spec_z.at[t, z_far, z_half:Z_TOTAL], z1_in.at[t, 1], z1_s.at[t, 1], z1_r.at[t, 1], lat_dev(x, z_down)),
         )
 
     def z2_copies(t):
         return (
-            send(spec.at[t, z_up], z2_in.at[t, 0], z2_s.at[t, 0], z2_r.at[t, 0], lat_dev(x, z_up)),
-            send(spec.at[t, z_down], z2_in.at[t, 1], z2_s.at[t, 1], z2_r.at[t, 1], lat_dev(x, z_down)),
-        )
-
-    def x_copy(t, source, to):
-        n, first = UNITS[to], OFFSETS[to]
+            send(spec_z.at[t, z_up], z2_in.at[t, 0], z2_s.at[t, 0], z2_r.at[t, 0], lat_dev(x, z_up)),
+            send(spec_z.at[t, z_down], z2_in.at[t, 1], z2_s.at[t, 1], z2_r.at[t, 1], lat_dev(x, z_down)),
+        )
+
+    def x1_copies(t):
+        return (
+            send(spec_x.at[t, x_far, 0:2], x1_in.at[t, 0], x1_s.at[t, 0], x1_r.at[t, 0], lat_dev(x_up, z)),
+            send(spec_x.at[t, x_far, 2:4], x1_in.at[t, 1], x1_s.at[t, 1], x1_r.at[t, 1], lat_dev(x_down, z)),
+        )
+
+    def x2_copies(t):
+        return (
+            send(spec_x.at[t, x_up], x2_in.at[t, 0], x2_s.at[t, 0], x2_r.at[t, 0], lat_dev(x_up, z)),
+            send(spec_x.at[t, x_down], x2_in.at[t, 1], x2_s.at[t, 1], x2_r.at[t, 1], lat_dev(x_down, z)),
+        )
+
+    def zx_copy(t, source, to):
+        n, first = Z_UNITS[to], Z_OFFSETS[to]
         return send(
-            spec.at[t, z, first : first + n], x_in.at[t, source, 0:n], x_s.at[t, to], x_r.at[t, source], lat_dev(to, z)
-        )
+            spec_z.at[t, z, first : first + n], zx_in.at[t, source, 0:n], zx_s.at[t, to], zx_r.at[t, source], lat_dev(to, z)
+        )
+
+    def xz_copies(t):
+        copies = []
+        for step in range(1, 4):
+            to = lax.rem(z + step, 4)
+            copies.append(
+                send(spec_x.at[t, x, to], xz_in.at[t, step - 1], xz_s.at[t, step - 1], xz_r.at[t, step - 1], lat_dev(x, to))
+            )
+        return copies
 
     for t in range(CHUNKS):
         table_copy(t).start()
@@ -135,10 +160,9 @@
         leg_copy(t).start()
 
     barrier = pltpu.get_barrier_semaphore()
-    for dev in (lon_dev(y, 1 - core), lon_dev(y_up, core), lon_dev(y_down, core), lat_dev(x, z_up), lat_dev(x, z_down)):
-        pl.semaphore_signal(barrier, inc=1, device_id=dev, device_id_type=pl.DeviceIdType.MESH)
-    for step in range(1, 4):
-        dev = lat_dev(lax.rem(x + step, 4), z)
+    neighbours = [lon_dev(y, 1 - core), lon_dev(y_up, core), lon_dev(y_down, core)]
+    neighbours += [lat_dev(x, to) for to in (z_up, z_far, z_down)] + [lat_dev(to, z) for to in (x_up, x_far, x_down)]
+    for dev in neighbours:
         pl.semaphore_signal(barrier, inc=1, device_id=dev, device_id_type=pl.DeviceIdType.MESH)
 
     def fields(step, carry):
@@ -162,7 +186,7 @@
 
     lax.fori_loop(0, 8, fields, 0)
 
-    pl.semaphore_wait(barrier, 8)
+    pl.semaphore_wait(barrier, len(neighbours))
 
     def analyse(t):
         slot = lax.rem(t, 2)
@@ -236,56 +260,77 @@
             n = UNITS[ox]
             right = leg[slot, owner, :, :, 0 : 128 * n].reshape(128, 128 * n)
             value = jnp.dot(left, right, preferred_element_type=jnp.float32)
-            for unit in range(n):
-                spec[t, oz, OFFSETS[ox] + unit] = value[:, unit * 128 : unit * 128 + 128]
-        for copy in z1_copies(t):
+            for unit in range(n - 1):
+                spec_z[t, oz, Z_OFFSETS[ox] + unit] = value[:, unit * 128 : unit * 128 + 128]
+            spec_x[t, ox, oz] = value[:, (n - 1) * 128 : n * 128]
+        for copy in (*z1_copies(t), *x1_copies(t)):
             copy.start()
 
         @pl.when(t + 2 < CHUNKS)
         def _():
             leg_copy(t + 2).start()
 
-    def z_forward(t):
+    def forward(t):
         for copy in z1_copies(t):
             copy.wait_recv()
-        spec[t, z_up, 0:half] = spec[t, z_up, 0:half] + z1_in[t, 0]
-        spec[t, z_down, half:TOTAL] = spec[t, z_down, half:TOTAL] + z1_in[t, 1]
+        spec_z[t, z_up, 0:z_half] = spec_z[t, z_up, 0:z_half] + z1_in[t, 0]
+        spec_z[t, z_down, z_half:Z_TOTAL] = spec_z[t, z_down, z_half:Z_TOTAL] + z1_in[t, 1]
         for copy in z2_copies(t):
             copy.start()
-
-    def x_start(t):
+        for copy in x1_copies(t):
+            copy.wait_recv()
+        spec_x[t, x_up, 0:2] = spec_x[t, x_up, 0:2] + x1_in[t, 0]
+        spec_x[t, x_down, 2:4] = spec_x[t, x_down, 2:4] + x1_in[t, 1]
+        for copy in x2_copies(t):
+            copy.start()
+
+    def cross(t):
         for copy in z2_copies(t):
             copy.wait_recv()
-        spec[t, z] = spec[t, z] + (z2_in[t, 0] + z2_in[t, 1])
-        for to in range(4):
+        spec_z[t, z] = spec_z[t, z] + (z2_in[t, 0] + z2_in[t, 1])
+        for to in range(3):
 
             @pl.when(x != to)
             def _():
-                x_copy(t, x, to).start()
+                zx_copy(t, x, to).start()
+
+        for copy in x2_copies(t):
+            copy.wait_recv()
+        spec_x[t, x] = spec_x[t, x] + (x2_in[t, 0] + x2_in[t, 1])
+        for copy in xz_copies(t):
+            copy.start()
 
     def finish(t):
         order = r + LON_DEV * (CHUNKS * k + t)
+        lane = lax.broadcasted_iota(jnp.int32, (32, 128), 1)
+        for copy in xz_copies(t):
+            copy.wait_recv()
+
+        def write(unit, e, value):
+            inside = order + 2 * (lane + unit * 128) + e < WAVES
+            out_ref[t, :, pl.ds(e * 512 + unit * 128, 128)] = jnp.where(inside, value, jnp.zeros_like(value))
+
         for mine in range(4):
 
             @pl.when(x == mine)
             def _():
-                n, first = UNITS[mine], OFFSETS[mine]
+                n, first = Z_UNITS[mine], Z_OFFSETS[mine]
                 others = [source for source in range(4) if source != mine]
-                for source in others:
-                    x_copy(t, source, mine).wait_recv()
-                lane = lax.broadcasted_iota(jnp.int32, (32, 128), 1)
-                for unit in range(4):
-                    for e in range(2):
-                        lanes = pl.ds(e * 512 + unit * 128, 128)
-                        if unit >= n:
-                            out_ref[t, :, lanes] = jnp.zeros((32, 128), jnp.float32)
-                            continue
-                        rows = pl.ds(e * 32, 32)
-                        value = spec[t, z, first + unit, rows, :]
+                for source in others if n else ():
+                    zx_copy(t, source, mine).wait_recv()
+                for e in range(2):
+                    rows = pl.ds(e * 32, 32)
+                    for unit in range(n):
+                        value = spec_z[t, z, first + unit, rows, :]
                         for source in others:
-                            value = value + x_in[t, source, unit, rows, :]
-                        inside = order + 2 * (lane + unit * 128) + e < WAVES
-                        out_ref[t, :, lanes] = jnp.where(inside, value, jnp.zeros_like(value))
+                            value = value + zx_in[t, source, unit, rows, :]
+                        write(unit, e, value)
+                    value = spec_x[t, mine, z, rows, :]
+                    for step in range(3):
+                        value = value + xz_in[t, step, rows, :]
+                    write(n, e, value)
+                    for unit in range(n + 1, 4):
+                        out_ref[t, :, pl.ds(e * 512 + unit * 128, 128)] = jnp.zeros((32, 128), jnp.float32)
 
     def stage(run, t):
         @pl.when((t >= 0) & (t < CHUNKS))
@@ -296,9 +341,9 @@
         t = step - 2
         stage(y_forward, t)
         stage(project, t - 1)
-        stage(x_start, t - 2)
+        stage(cross, t - 2)
         stage(analyse, t + 2)
-        stage(z_forward, t - 1)
+        stage(forward, t - 1)
         stage(pair_sum, t + 2)
         stage(finish, t - 3)
         return carry
@@ -310,13 +355,14 @@
         def _():
             core_copy(t).wait_send()
 
-        for copy in (*y1_copies(t), *y2_copies(t), *z1_copies(t), *z2_copies(t)):
+        ring = (*y1_copies(t), *y2_copies(t), *z1_copies(t), *z2_copies(t), *x1_copies(t), *x2_copies(t))
+        for copy in (*ring, *xz_copies(t)):
             copy.wait_send()
-        for to in range(4):
+        for to in range(3):
 
             @pl.when(x != to)
             def _():
-                x_copy(t, x, to).wait_send()
+                zx_copy(t, x, to).wait_send()
 
         return carry
 
@@ -348,17 +394,21 @@
             pltpu.VMEM((CHUNKS, 2, 2, 16, ROWS), f32),
             pltpu.VMEM((512, 128), f32),
             pltpu.VMEM((2, 16, 64, 2, 512), bf16),
-            pltpu.VMEM((CHUNKS, 4, TOTAL, 64, 128), f32),
-            pltpu.VMEM((CHUNKS, 2, TOTAL // 2, 64, 128), f32),
-            pltpu.VMEM((CHUNKS, 2, TOTAL, 64, 128), f32),
+            pltpu.VMEM((CHUNKS, 4, Z_TOTAL, 64, 128), f32),
             pltpu.VMEM((CHUNKS, 4, 4, 64, 128), f32),
+            pltpu.VMEM((CHUNKS, 2, Z_TOTAL // 2, 64, 128), f32),
+            pltpu.VMEM((CHUNKS, 2, Z_TOTAL, 64, 128), f32),
+            pltpu.VMEM((CHUNKS, 4, 3, 64, 128), f32),
+            pltpu.VMEM((CHUNKS, 2, 2, 64, 128), f32),
+            pltpu.VMEM((CHUNKS, 2, 4, 64, 128), f32),
+            pltpu.VMEM((CHUNKS, 3, 64, 128), f32),
             dma((CHUNKS,)),
             dma((2,)),
             dma((CHUNKS,)),
             dma((CHUNKS,)),
-            *[dma((CHUNKS, 2)) for _ in range(8)],
-            dma((CHUNKS, 4)),
-            dma((CHUNKS, 4)),
+            *[dma((CHUNKS, 2)) for _ in range(12)],
+            *[dma((CHUNKS, 4)) for _ in range(2)],
+            *[dma((CHUNKS, 3)) for _ in range(2)],
         ],
         compiler_params=pltpu.CompilerParams(
             collective_id=0, has_side_effects=True, vmem_limit_bytes=62 * 2**20

time: 139 us -> 123 us (0.88)
  Pallas kernels: 136 us -> 119 us
    pallas_call x1, Pallas kernels: 136 us -> 119 us  [local(): pl.pallas_call(kernel, out_shape=jax.ShapeDtypeStruct((CHUNKS, 32, WAVES)...]
where the time goes in v2:
time: 123 us
  Pallas kernels  119 us (97%)
  local copies, waits for them, and re-layouts  3.08 us (3%)
    pallas_call x1, Pallas kernels, local(): pl.pallas_call(kernel, out_shape=jax.ShapeDtypeStruct((CHUNKS, 32, WAVES)...  119 us
    reshape x1, local copies, waits for them, and re-layouts, local(): return result.reshape(1, CHUNKS, 8, 2, 2, 2, 512)  3.08 us

profile of v2, /device:TPU:0, one launch (start us, length us, event | category | flops | bytes accessed | tf_op | source)
XLA Modules:
  0.0 122.5 jit_solution(9719754872190136187)
XLA Ops:
  0.0 119.4 %spectral.1 = f32[8,32,1024]{2,1,0:T(8,128)} custom-call(bf16[12,2,2,64,512]{4,3,2,1,0:T(8,128)(2,1)} %grid_ref.1, f32[8,8,2,16,512]{4,3,2,1,0:T(8,128)} %constant.2.clone.table_ref, bf16[16,8,64,2,512]{4,3,2,1,0:T(2,128)(2,1)} %bitcast.1), custom_call_target="tpu_custom_call" | custom-call | tf_op jit(solution)/shard_map/spectral/pallas_call | solution.py:376
  119.4 3.1 %reshape.7 = f32[1,8,8,2,2,2,512]{6,5,4,3,2,1,0:T(2,128)} reshape(f32[8,32,1024]{2,1,0:T(8,128)} %spectral.1) | data formatting | bytes 2097152 | tf_op jit(solution)/shard_map/reshape | solution.py:418

commit v3 on v2

--- a/solution.py
+++ b/solution.py
@@ -11,8 +11,10 @@
 LON_DEV = 8
 LAT_DEV = 16
 LON_LOCAL = NLON // LON_DEV
-ROWS = 2048
+ROWS = 1024
 CHUNKS = 8
+LEVELS = 2
+STEPS = CHUNKS * LEVELS
 UNITS = (4, 3, 2, 1)
 Z_UNITS = (3, 2, 1, 0)
 Z_OFFSETS = (0, 3, 5, 6)
@@ -64,9 +66,9 @@
 
 def kernel(
     grid_ref, table_ref, leg_ref, out_ref,
-    t_hi, t_lo, mix, table, phases, part, paired, y1_in, y2_in, fold, leg,
+    grid, t_hi, t_lo, mix, table, phases, part, paired, y1_in, y2_in, fold, leg,
     spec_z, spec_x, z1_in, z2_in, zx_in, x1_in, x2_in, xz_in,
-    table_sem, leg_sem, core_s, core_r, y1_s, y1_r, y2_s, y2_r,
+    grid_sem, table_sem, leg_sem, core_s, core_r, y1_s, y1_r, y2_s, y2_r,
     z1_s, z1_r, z2_s, z2_r, x1_s, x1_r, x2_s, x2_r, zx_s, zx_r, xz_s, xz_r,
 ):
     r = lax.axis_index("lon")
@@ -92,9 +94,12 @@
     def table_copy(t):
         return pltpu.make_async_copy(table_ref.at[t], table.at[t], table_sem.at[t])
 
-    def leg_copy(t):
-        slot = lax.rem(t, 2)
-        return pltpu.make_async_copy(leg_ref.at[:, t], leg.at[slot], leg_sem.at[slot])
+    def leg_copy(i):
+        slot = lax.rem(i, 2)
+        return pltpu.make_async_copy(leg_ref.at[:, i], leg.at[slot], leg_sem.at[slot])
+
+    def grid_copy(level):
+        return pltpu.make_async_copy(grid_ref.at[:, level], grid.at[level], grid_sem.at[level])
 
     def core_copy(t):
         return send(
@@ -154,10 +159,13 @@
             )
         return copies
 
-    for t in range(CHUNKS):
-        table_copy(t).start()
-    for t in range(2):
-        leg_copy(t).start()
+    grid_copy(0).start()
+    table_copy(0).start()
+    grid_copy(1).start()
+    for i in range(2):
+        leg_copy(i).start()
+    for i in range(1, CHUNKS):
+        table_copy(i).start()
 
     barrier = pltpu.get_barrier_semaphore()
     neighbours = [lon_dev(y, 1 - core), lon_dev(y_up, core), lon_dev(y_down, core)]
@@ -165,59 +173,62 @@
     for dev in neighbours:
         pl.semaphore_signal(barrier, inc=1, device_id=dev, device_id_type=pl.DeviceIdType.MESH)
 
-    def fields(step, carry):
-        level, block = step // 4, lax.rem(step, 4)
-        first = pl.multiple_of(block * 16, 16)
-        for lane in range(4):
-            lanes = pl.ds(lane * 128, 128)
-            north, south = (
-                tendencies([grid_ref[f, level, h, pl.ds(first, 16), lanes].astype(jnp.float32) for f in range(12)])
-                for h in range(2)
-            )
-            for t in range(8):
-                mix[lane * 8 + t, pl.ds(0, 16, stride=2), :] = north[t] + south[t]
-                mix[lane * 8 + t, pl.ds(1, 16, stride=2), :] = north[t] - south[t]
-            for t in range(8):
-                high, low = split_bf16(mix[lane * 8 + t])
-                at = pl.multiple_of((2 * t + level) * 128 + block * 32, 32)
-                t_hi[pl.ds(at, 32), lanes] = high
-                t_lo[pl.ds(at, 32), lanes] = low
-        return carry
-
-    lax.fori_loop(0, 8, fields, 0)
-
+    def fields(level):
+        grid_copy(level).wait()
+
+        def rows16(block, carry):
+            first = pl.multiple_of(block * 16, 16)
+            for lane in range(4):
+                lanes = pl.ds(lane * 128, 128)
+                north, south = (
+                    tendencies([grid[level, f, h, pl.ds(first, 16), lanes].astype(jnp.float32) for f in range(12)])
+                    for h in range(2)
+                )
+                for t in range(8):
+                    mix[lane * 8 + t, pl.ds(0, 16, stride=2), :] = north[t] + south[t]
+                    mix[lane * 8 + t, pl.ds(1, 16, stride=2), :] = north[t] - south[t]
+                for t in range(8):
+                    high, low = split_bf16(mix[lane * 8 + t])
+                    at = pl.multiple_of(t * 128 + block * 32, 32)
+                    t_hi[level, pl.ds(at, 32), lanes] = high
+                    t_lo[level, pl.ds(at, 32), lanes] = low
+            return carry
+
+        lax.fori_loop(0, 4, rows16, 0)
+
+    fields(0)
     pl.semaphore_wait(barrier, len(neighbours))
 
     def analyse(t):
-        slot = lax.rem(t, 2)
-        table_copy(t).wait()
-
-        def rotate(block, carry):
-            q = 2 * lax.rem(block, 4) + block // 4
-            c, s = eighth_cos(r * q), eighth_cos(r * q + 6)
-            real, imag = table[t, block, 0], table[t, block, 1]
-            for part_index, value in enumerate((real * c + imag * s, imag * c - real * s)):
-                high, low = split_bf16(value)
-                at = pl.multiple_of(block * 32 + part_index * 16, 16)
-                phases[pl.ds(at, 16), :] = high
-                phases[pl.ds(at + 256, 16), :] = low
-            return carry
-
-        lax.fori_loop(0, 8, rotate, 0)
+        slot, i, level = lax.rem(t, 2), t // LEVELS, lax.rem(t, LEVELS)
+
+        @pl.when(level == 0)
+        def _():
+            table_copy(i).wait()
+
+            def rotate(block, carry):
+                q = 2 * lax.rem(block, 4) + block // 4
+                c, s = eighth_cos(r * q), eighth_cos(r * q + 6)
+                real, imag = table[i, block, 0], table[i, block, 1]
+                for part_index, value in enumerate((real * c + imag * s, imag * c - real * s)):
+                    high, low = split_bf16(value)
+                    at = pl.multiple_of(block * 32 + part_index * 16, 16)
+                    phases[pl.ds(at, 16), :] = high
+                    phases[pl.ds(at + 256, 16), :] = low
+                return carry
+
+            lax.fori_loop(0, 8, rotate, 0)
 
         @pl.when(t >= 2)
         def _():
             core_copy(t - 2).wait_send()
 
-        def columns(n, carry):
-            rows = pl.ds(pl.multiple_of(n * 256, 256), 256)
-            both = lax.dot_general(phases[...], t_hi[rows, :], NT, preferred_element_type=jnp.float32)
-            rest = lax.dot_general(phases[0:256, :], t_lo[rows, :], NT, preferred_element_type=jnp.float32)
+        for n in range(ROWS // 256):
+            rows = pl.ds(n * 256, 256)
+            both = lax.dot_general(phases[...], t_hi[level, rows, :], NT, preferred_element_type=jnp.float32)
+            rest = lax.dot_general(phases[0:256, :], t_lo[level, rows, :], NT, preferred_element_type=jnp.float32)
             value = both[0:256] + (both[256:512] + rest)
             part[slot, :, :, :, :, rows] = value.reshape(2, 4, 2, 16, 256)
-            return carry
-
-        lax.fori_loop(0, 8, columns, 0)
         core_copy(t).start()
 
     def pair_sum(t):
@@ -242,19 +253,24 @@
             copy.start()
 
     def project(t):
-        slot = lax.rem(t, 2)
+        i, level = t // LEVELS, lax.rem(t, LEVELS)
+        slot = lax.rem(i, 2)
         for copy in y2_copies(t):
             copy.wait_recv()
         for c in range(2):
-            for tl in range(16):
-                lanes = pl.ds(tl * 128, 128)
+            for f in range(8):
+                lanes = pl.ds(f * 128, 128)
                 value = paired[t, y, c, :, lanes] + (y2_in[t, 0, c, :, lanes] + y2_in[t, 1, c, :, lanes])
-                fold[pl.ds(tl * 2 + c, 16, stride=32), :] = value
-        leg_copy(t).wait()
-        even = lax.rem(lax.broadcasted_iota(jnp.int32, (32, 128), 1), 2) == 0
+                fold[pl.ds(c * 8 + f, 16, stride=16), :] = value
+
+        @pl.when(level == 0)
+        def _():
+            leg_copy(i).wait()
+
+        even = lax.rem(lax.broadcasted_iota(jnp.int32, (16, 128), 1), 2) == 0
         for owner in range(LAT_DEV):
             ox, oz = owner // 4, owner % 4
-            rows = fold[owner * 32 : owner * 32 + 32, :]
+            rows = fold[owner * 16 : owner * 16 + 16, :]
             zero = jnp.zeros_like(rows)
             left = jnp.concatenate([jnp.where(even, rows, zero), jnp.where(even, zero, rows)], 0).astype(jnp.bfloat16)
             n = UNITS[ox]
@@ -266,9 +282,9 @@
         for copy in (*z1_copies(t), *x1_copies(t)):
             copy.start()
 
-        @pl.when(t + 2 < CHUNKS)
-        def _():
-            leg_copy(t + 2).start()
+        @pl.when((level == LEVELS - 1) & (i + 2 < CHUNKS))
+        def _():
+            leg_copy(i + 2).start()
 
     def forward(t):
         for copy in z1_copies(t):
@@ -301,14 +317,15 @@
             copy.start()
 
     def finish(t):
-        order = r + LON_DEV * (CHUNKS * k + t)
-        lane = lax.broadcasted_iota(jnp.int32, (32, 128), 1)
+        i, level = t // LEVELS, lax.rem(t, LEVELS)
+        order = r + LON_DEV * (CHUNKS * k + i)
+        lane = lax.broadcasted_iota(jnp.int32, (16, 128), 1)
         for copy in xz_copies(t):
             copy.wait_recv()
 
         def write(unit, e, value):
             inside = order + 2 * (lane + unit * 128) + e < WAVES
-            out_ref[t, :, pl.ds(e * 512 + unit * 128, 128)] = jnp.where(inside, value, jnp.zeros_like(value))
+            out_ref[i, level, :, pl.ds(e * 512 + unit * 128, 128)] = jnp.where(inside, value, jnp.zeros_like(value))
 
         for mine in range(4):
 
@@ -319,7 +336,7 @@
                 for source in others if n else ():
                     zx_copy(t, source, mine).wait_recv()
                 for e in range(2):
-                    rows = pl.ds(e * 32, 32)
+                    rows = pl.ds(e * 16, 16)
                     for unit in range(n):
                         value = spec_z[t, z, first + unit, rows, :]
                         for source in others:
@@ -330,28 +347,33 @@
                         value = value + xz_in[t, step, rows, :]
                     write(n, e, value)
                     for unit in range(n + 1, 4):
-                        out_ref[t, :, pl.ds(e * 512 + unit * 128, 128)] = jnp.zeros((32, 128), jnp.float32)
+                        out_ref[i, level, :, pl.ds(e * 512 + unit * 128, 128)] = jnp.zeros((16, 128), jnp.float32)
 
     def stage(run, t):
-        @pl.when((t >= 0) & (t < CHUNKS))
+        @pl.when((t >= 0) & (t < STEPS))
         def _():
             run(t)
 
     def steps(step, carry):
-        t = step - 2
+        t = step - 3
         stage(y_forward, t)
         stage(project, t - 1)
-        stage(cross, t - 2)
-        stage(analyse, t + 2)
-        stage(forward, t - 1)
+        stage(forward, t - 2)
+        stage(cross, t - 3)
+        stage(finish, t - 4)
         stage(pair_sum, t + 2)
-        stage(finish, t - 3)
+
+        @pl.when(t == -2)
+        def _():
+            fields(1)
+
+        stage(analyse, t + 3)
         return carry
 
-    lax.fori_loop(0, CHUNKS + 5, steps, 0)
+    lax.fori_loop(0, STEPS + 7, steps, 0)
 
     def drain(t, carry):
-        @pl.when(t >= CHUNKS - 2)
+        @pl.when(t >= STEPS - 2)
         def _():
             core_copy(t).wait_send()
 
@@ -366,7 +388,7 @@
 
         return carry
 
-    lax.fori_loop(0, CHUNKS, drain, 0)
+    lax.fori_loop(0, STEPS, drain, 0)
 
 
 def local(grid, legendre):
@@ -375,47 +397,46 @@
     dma = pltpu.SemaphoreType.DMA
     result = pl.pallas_call(
         kernel,
-        out_shape=jax.ShapeDtypeStruct((CHUNKS, 32, WAVES), f32),
-        in_specs=[
-            pl.BlockSpec(memory_space=pltpu.VMEM),
-            pl.BlockSpec(memory_space=pl.ANY),
-            pl.BlockSpec(memory_space=pl.ANY),
-        ],
+        out_shape=jax.ShapeDtypeStruct((CHUNKS, LEVELS, 16, WAVES), f32),
+        in_specs=[pl.BlockSpec(memory_space=pl.ANY)] * 3,
         out_specs=pl.BlockSpec(memory_space=pltpu.VMEM),
         scratch_shapes=[
-            pltpu.VMEM((ROWS, LON_LOCAL), bf16),
-            pltpu.VMEM((ROWS, LON_LOCAL), bf16),
+            pltpu.VMEM((LEVELS, 12, 2, 64, LON_LOCAL), bf16),
+            pltpu.VMEM((LEVELS, ROWS, LON_LOCAL), bf16),
+            pltpu.VMEM((LEVELS, ROWS, LON_LOCAL), bf16),
             pltpu.VMEM((32, 32, 128), f32),
             pltpu.VMEM((CHUNKS, 8, 2, 16, LON_LOCAL), f32),
             pltpu.VMEM((512, LON_LOCAL), bf16),
             pltpu.VMEM((2, 2, 4, 2, 16, ROWS), f32),
-            pltpu.VMEM((CHUNKS, 4, 2, 16, ROWS), f32),
-            pltpu.VMEM((CHUNKS, 2, 16, ROWS), f32),
-            pltpu.VMEM((CHUNKS, 2, 2, 16, ROWS), f32),
-            pltpu.VMEM((512, 128), f32),
+            pltpu.VMEM((STEPS, 4, 2, 16, ROWS), f32),
+            pltpu.VMEM((STEPS, 2, 16, ROWS), f32),
+            pltpu.VMEM((STEPS, 2, 2, 16, ROWS), f32),
+            pltpu.VMEM((256, 128), f32),
             pltpu.VMEM((2, 16, 64, 2, 512), bf16),
-            pltpu.VMEM((CHUNKS, 4, Z_TOTAL, 64, 128), f32),
-            pltpu.VMEM((CHUNKS, 4, 4, 64, 128), f32),
-            pltpu.VMEM((CHUNKS, 2, Z_TOTAL // 2, 64, 128), f32),
-            pltpu.VMEM((CHUNKS, 2, Z_TOTAL, 64, 128), f32),
-            pltpu.VMEM((CHUNKS, 4, 3, 64, 128), f32),
-            pltpu.VMEM((CHUNKS, 2, 2, 64, 128), f32),
-            pltpu.VMEM((CHUNKS, 2, 4, 64, 128), f32),
-            pltpu.VMEM((CHUNKS, 3, 64, 128), f32),
+            pltpu.VMEM((STEPS, 4, Z_TOTAL, 32, 128), f32),
+            pltpu.VMEM((STEPS, 4, 4, 32, 128), f32),
+            pltpu.VMEM((STEPS, 2, Z_TOTAL // 2, 32, 128), f32),
+            pltpu.VMEM((STEPS, 2, Z_TOTAL, 32, 128), f32),
+            pltpu.VMEM((STEPS, 4, 3, 32, 128), f32),
+            pltpu.VMEM((STEPS, 2, 2, 32, 128), f32),
+            pltpu.VMEM((STEPS, 2, 4, 32, 128), f32),
+            pltpu.VMEM((STEPS, 3, 32, 128), f32),
+            dma((LEVELS,)),
             dma((CHUNKS,)),
             dma((2,)),
-            dma((CHUNKS,)),
-            dma((CHUNKS,)),
-            *[dma((CHUNKS, 2)) for _ in range(12)],
-            *[dma((CHUNKS, 4)) for _ in range(2)],
-            *[dma((CHUNKS, 3)) for _ in range(2)],
+            dma((STEPS,)),
+            dma((STEPS,)),
+            *[dma((STEPS, 2)) for _ in range(12)],
+            *[dma((STEPS, 4)) for _ in range(2)],
+            *[dma((STEPS, 3)) for _ in range(2)],
         ],
         compiler_params=pltpu.CompilerParams(
             collective_id=0, has_side_effects=True, vmem_limit_bytes=62 * 2**20
         ),
         name="spectral",
     )(grid, table, legendre.reshape(LAT_DEV, CHUNKS, 64, 2, 512))
-    return result.reshape(1, CHUNKS, 8, 2, 2, 2, 512)
+    spectral = result.reshape(1, CHUNKS, LEVELS, 2, 8, 2, WAVES // 2)
+    return jnp.transpose(spectral, (0, 1, 4, 2, 3, 5, 6))
 
 
 def solution(mesh):

time: 123 us -> 109 us (0.89)
  Pallas kernels: 119 us -> 106 us
    pallas_call x1, Pallas kernels: 119 us -> 106 us  [local(): pl.pallas_call(kernel, out_shape=jax.ShapeDtypeStruct((CHUNKS, LEVELS, 16...]
where the time goes in v3:
time: 109 us
  Pallas kernels  106 us (97%)
  local copies, waits for them, and re-layouts  3.01 us (3%)
    pallas_call x1, Pallas kernels, local(): pl.pallas_call(kernel, out_shape=jax.ShapeDtypeStruct((CHUNKS, LEVELS, 16...  106 us
    reshape x1, local copies, waits for them, and re-layouts, local(): spectral = result.reshape(1, CHUNKS, LEVELS, 2, 8, 2, WAVES // 2)  3.01 us

profile of v3, /device:TPU:0, one launch (start us, length us, event | category | flops | bytes accessed | tf_op | source)
XLA Modules:
  0.0 108.8 jit_solution(12520991472312701875)
XLA Ops:
  0.0 105.8 %spectral.1 = f32[8,2,16,1024]{3,2,1,0:T(8,128)} custom-call(bf16[12,2,2,64,512]{4,3,2,1,0:T(8,128)(2,1)} %grid_ref.1, f32[8,8,2,16,512]{4,3,2,1,0:T(8,128)} %constant.2.clone.table_ref, bf16[16,8,64,2,512]{4,3,2,1,0:T(2,128)(2,1)} %bitcast.5), custom_call_target="tpu_custom_call" | custom-call | tf_op jit(solution)/shard_map/spectral/pallas_call | solution.py:398
  105.8 3.0 %copy.6 = f32[1,8,2,2,8,2,512]{6,5,3,2,4,1,0:T(2,128)} copy(f32[1,8,2,2,8,2,512]{6,4,5,3,2,1,0:T(8,128)} %bitcast.6) | data formatting | bytes 2097152 | tf_op jit(solution)/shard_map/reshape | solution.py:438

commit v4 on v3

--- a/solution.py
+++ b/solution.py
@@ -19,6 +19,10 @@
 Z_UNITS = (3, 2, 1, 0)
 Z_OFFSETS = (0, 3, 5, 6)
 Z_TOTAL = 6
+X_ROWS = (32, 32, 16, 16)
+X_OFFSETS = (0, 32, 64, 80)
+X_TOTAL = 96
+X_HALF = X_TOTAL // 2
 ADIABATIC = 0.286
 ROOT_HALF = 0.5**0.5
 
@@ -67,8 +71,8 @@
 def kernel(
     grid_ref, table_ref, leg_ref, out_ref,
     grid, t_hi, t_lo, mix, table, phases, part, paired, y1_in, y2_in, fold, leg,
-    spec_z, spec_x, z1_in, z2_in, zx_in, x1_in, x2_in, xz_in,
-    grid_sem, table_sem, leg_sem, core_s, core_r, y1_s, y1_r, y2_s, y2_r,
+    spec_z, spec_x, z1_in, z2_in, zx_in, x1_in, x2_in, xz_in, result,
+    grid_sem, out_sem, table_sem, leg_sem, core_s, core_r, y1_s, y1_r, y2_s, y2_r,
     z1_s, z1_r, z2_s, z2_r, x1_s, x1_r, x2_s, x2_r, zx_s, zx_r, xz_s, xz_r,
 ):
     r = lax.axis_index("lon")
@@ -94,9 +98,13 @@
     def table_copy(t):
         return pltpu.make_async_copy(table_ref.at[t], table.at[t], table_sem.at[t])
 
-    def leg_copy(i):
-        slot = lax.rem(i, 2)
-        return pltpu.make_async_copy(leg_ref.at[:, i], leg.at[slot], leg_sem.at[slot])
+    def leg_copy(t):
+        slot = lax.rem(t, 2)
+        return pltpu.make_async_copy(leg_ref.at[:, lax.rem(t, CHUNKS)], leg.at[slot], leg_sem.at[slot])
+
+    def out_copy(t):
+        at = (lax.rem(t, CHUNKS), t // CHUNKS)
+        return pltpu.make_async_copy(result.at[at], out_ref.at[at], out_sem.at[t])
 
     def grid_copy(level):
         return pltpu.make_async_copy(grid_ref.at[:, level], grid.at[level], grid_sem.at[level])
@@ -134,8 +142,8 @@
 
     def x1_copies(t):
         return (
-            send(spec_x.at[t, x_far, 0:2], x1_in.at[t, 0], x1_s.at[t, 0], x1_r.at[t, 0], lat_dev(x_up, z)),
-            send(spec_x.at[t, x_far, 2:4], x1_in.at[t, 1], x1_s.at[t, 1], x1_r.at[t, 1], lat_dev(x_down, z)),
+            send(spec_x.at[t, x_far, 0:X_HALF], x1_in.at[t, 0], x1_s.at[t, 0], x1_r.at[t, 0], lat_dev(x_up, z)),
+            send(spec_x.at[t, x_far, X_HALF:X_TOTAL], x1_in.at[t, 1], x1_s.at[t, 1], x1_r.at[t, 1], lat_dev(x_down, z)),
         )
 
     def x2_copies(t):
@@ -150,17 +158,14 @@
             spec_z.at[t, z, first : first + n], zx_in.at[t, source, 0:n], zx_s.at[t, to], zx_r.at[t, source], lat_dev(to, z)
         )
 
-    def xz_copies(t):
-        copies = []
-        for step in range(1, 4):
-            to = lax.rem(z + step, 4)
-            copies.append(
-                send(spec_x.at[t, x, to], xz_in.at[t, step - 1], xz_s.at[t, step - 1], xz_r.at[t, step - 1], lat_dev(x, to))
-            )
-        return copies
-
+    def xz_copy(t, source, to):
+        n, first = X_ROWS[to], X_OFFSETS[to]
+        return send(
+            spec_x.at[t, x, first : first + n], xz_in.at[t, source, 0:n], xz_s.at[t, to], xz_r.at[t, source], lat_dev(x, to)
+        )
+
+    table_copy(0).start()
     grid_copy(0).start()
-    table_copy(0).start()
     grid_copy(1).start()
     for i in range(2):
         leg_copy(i).start()
@@ -196,28 +201,33 @@
 
         lax.fori_loop(0, 4, rows16, 0)
 
+    def rotate(t):
+        i = lax.rem(t, CHUNKS)
+
+        @pl.when(t < CHUNKS)
+        def _():
+            table_copy(i).wait()
+
+        def block_of(block, carry):
+            q = 2 * lax.rem(block, 4) + block // 4
+            c, s = eighth_cos(r * q), eighth_cos(r * q + 6)
+            real, imag = table[i, block, 0], table[i, block, 1]
+            for part_index, value in enumerate((real * c + imag * s, imag * c - real * s)):
+                high, low = split_bf16(value)
+                at = pl.multiple_of(block * 32 + part_index * 16, 16)
+                phases[pl.ds(at, 16), :] = high
+                phases[pl.ds(at + 256, 16), :] = low
+            return carry
+
+        lax.fori_loop(0, 8, block_of, 0)
+
+    rotate(0)
     fields(0)
+
     pl.semaphore_wait(barrier, len(neighbours))
 
     def analyse(t):
-        slot, i, level = lax.rem(t, 2), t // LEVELS, lax.rem(t, LEVELS)
-
-        @pl.when(level == 0)
-        def _():
-            table_copy(i).wait()
-
-            def rotate(block, carry):
-                q = 2 * lax.rem(block, 4) + block // 4
-                c, s = eighth_cos(r * q), eighth_cos(r * q + 6)
-                real, imag = table[i, block, 0], table[i, block, 1]
-                for part_index, value in enumerate((real * c + imag * s, imag * c - real * s)):
-                    high, low = split_bf16(value)
-                    at = pl.multiple_of(block * 32 + part_index * 16, 16)
-                    phases[pl.ds(at, 16), :] = high
-                    phases[pl.ds(at + 256, 16), :] = low
-                return carry
-
-            lax.fori_loop(0, 8, rotate, 0)
+        slot, level = lax.rem(t, 2), t // CHUNKS
 
         @pl.when(t >= 2)
         def _():
@@ -231,6 +241,10 @@
             part[slot, :, :, :, :, rows] = value.reshape(2, 4, 2, 16, 256)
         core_copy(t).start()
 
+        @pl.when(t + 1 < STEPS)
+        def _():
+            rotate(t + 1)
+
     def pair_sum(t):
         slot = lax.rem(t, 2)
         core_copy(t).wait_recv()
@@ -253,8 +267,7 @@
             copy.start()
 
     def project(t):
-        i, level = t // LEVELS, lax.rem(t, LEVELS)
-        slot = lax.rem(i, 2)
+        slot = lax.rem(t, 2)
         for copy in y2_copies(t):
             copy.wait_recv()
         for c in range(2):
@@ -263,11 +276,9 @@
                 value = paired[t, y, c, :, lanes] + (y2_in[t, 0, c, :, lanes] + y2_in[t, 1, c, :, lanes])
                 fold[pl.ds(c * 8 + f, 16, stride=16), :] = value
 
-        @pl.when(level == 0)
-        def _():
-            leg_copy(i).wait()
-
-        even = lax.rem(lax.broadcasted_iota(jnp.int32, (16, 128), 1), 2) == 0
+        leg_copy(t).wait()
+        lane = lax.broadcasted_iota(jnp.int32, (16, 128), 1)
+        even, low_half = lax.rem(lane, 2) == 0, lane < 64
         for owner in range(LAT_DEV):
             ox, oz = owner // 4, owner % 4
             rows = fold[owner * 16 : owner * 16 + 16, :]
@@ -278,13 +289,17 @@
             value = jnp.dot(left, right, preferred_element_type=jnp.float32)
             for unit in range(n - 1):
                 spec_z[t, oz, Z_OFFSETS[ox] + unit] = value[:, unit * 128 : unit * 128 + 128]
-            spec_x[t, ox, oz] = value[:, (n - 1) * 128 : n * 128]
+            last, first = value[:, (n - 1) * 128 : n * 128], X_OFFSETS[oz]
+            if X_ROWS[oz] == 32:
+                spec_x[t, ox, first : first + 32, :] = last
+            else:
+                spec_x[t, ox, first : first + 16, :] = jnp.where(low_half, last[0:16], pltpu.roll(last[16:32], 64, 1))
         for copy in (*z1_copies(t), *x1_copies(t)):
             copy.start()
 
-        @pl.when((level == LEVELS - 1) & (i + 2 < CHUNKS))
-        def _():
-            leg_copy(i + 2).start()
+        @pl.when(t + 2 < STEPS)
+        def _():
+            leg_copy(t + 2).start()
 
     def forward(t):
         for copy in z1_copies(t):
@@ -295,8 +310,8 @@
             copy.start()
         for copy in x1_copies(t):
             copy.wait_recv()
-        spec_x[t, x_up, 0:2] = spec_x[t, x_up, 0:2] + x1_in[t, 0]
-        spec_x[t, x_down, 2:4] = spec_x[t, x_down, 2:4] + x1_in[t, 1]
+        spec_x[t, x_up, 0:X_HALF] = spec_x[t, x_up, 0:X_HALF] + x1_in[t, 0]
+        spec_x[t, x_down, X_HALF:X_TOTAL] = spec_x[t, x_down, X_HALF:X_TOTAL] + x1_in[t, 1]
         for copy in x2_copies(t):
             copy.start()
 
@@ -313,19 +328,21 @@
         for copy in x2_copies(t):
             copy.wait_recv()
         spec_x[t, x] = spec_x[t, x] + (x2_in[t, 0] + x2_in[t, 1])
-        for copy in xz_copies(t):
-            copy.start()
+        for to in range(4):
+
+            @pl.when(z != to)
+            def _():
+                xz_copy(t, z, to).start()
 
     def finish(t):
-        i, level = t // LEVELS, lax.rem(t, LEVELS)
+        i, level = lax.rem(t, CHUNKS), t // CHUNKS
         order = r + LON_DEV * (CHUNKS * k + i)
         lane = lax.broadcasted_iota(jnp.int32, (16, 128), 1)
-        for copy in xz_copies(t):
-            copy.wait_recv()
-
         def write(unit, e, value):
             inside = order + 2 * (lane + unit * 128) + e < WAVES
-            out_ref[i, level, :, pl.ds(e * 512 + unit * 128, 128)] = jnp.where(inside, value, jnp.zeros_like(value))
+            first = e * 512 + unit * 128
+            first = first if isinstance(first, int) else pl.multiple_of(first, 128)
+            result[i, level, :, pl.ds(first, 128)] = jnp.where(inside, value, jnp.zeros_like(value))
 
         for mine in range(4):
 
@@ -342,12 +359,24 @@
                         for source in others:
                             value = value + zx_in[t, source, unit, rows, :]
                         write(unit, e, value)
-                    value = spec_x[t, mine, z, rows, :]
-                    for step in range(3):
-                        value = value + xz_in[t, step, rows, :]
-                    write(n, e, value)
                     for unit in range(n + 1, 4):
-                        out_ref[i, level, :, pl.ds(e * 512 + unit * 128, 128)] = jnp.zeros((16, 128), jnp.float32)
+                        result[i, level, :, pl.ds(e * 512 + unit * 128, 128)] = jnp.zeros((16, 128), jnp.float32)
+
+        for mine in range(4):
+
+            @pl.when(z == mine)
+            def _():
+                n, first = X_ROWS[mine], X_OFFSETS[mine]
+                others = [source for source in range(4) if source != mine]
+                for source in others:
+                    xz_copy(t, source, mine).wait_recv()
+                value = spec_x[t, x, first : first + n, :]
+                for source in others:
+                    value = value + xz_in[t, source, 0:n, :]
+                write(3 - x, 0, value[0:16])
+                write(3 - x, 1, value[16:32] if n == 32 else pltpu.roll(value, 64, 1))
+
+        out_copy(t).start()
 
     def stage(run, t):
         @pl.when((t >= 0) & (t < STEPS))
@@ -355,22 +384,22 @@
             run(t)
 
     def steps(step, carry):
-        t = step - 3
+        t = step - 4
         stage(y_forward, t)
         stage(project, t - 1)
         stage(forward, t - 2)
         stage(cross, t - 3)
+        stage(pair_sum, t + 2)
         stage(finish, t - 4)
-        stage(pair_sum, t + 2)
-
-        @pl.when(t == -2)
+        stage(analyse, t + 4)
+
+        @pl.when(t == 0)
         def _():
             fields(1)
 
-        stage(analyse, t + 3)
         return carry
 
-    lax.fori_loop(0, STEPS + 7, steps, 0)
+    lax.fori_loop(0, STEPS + 8, steps, 0)
 
     def drain(t, carry):
         @pl.when(t >= STEPS - 2)
@@ -378,8 +407,15 @@
             core_copy(t).wait_send()
 
         ring = (*y1_copies(t), *y2_copies(t), *z1_copies(t), *z2_copies(t), *x1_copies(t), *x2_copies(t))
-        for copy in (*ring, *xz_copies(t)):
+        for copy in ring:
             copy.wait_send()
+        out_copy(t).wait()
+        for to in range(4):
+
+            @pl.when(z != to)
+            def _():
+                xz_copy(t, z, to).wait_send()
+
         for to in range(3):
 
             @pl.when(x != to)
@@ -399,7 +435,7 @@
         kernel,
         out_shape=jax.ShapeDtypeStruct((CHUNKS, LEVELS, 16, WAVES), f32),
         in_specs=[pl.BlockSpec(memory_space=pl.ANY)] * 3,
-        out_specs=pl.BlockSpec(memory_space=pltpu.VMEM),
+        out_specs=pl.BlockSpec(memory_space=pl.ANY),
         scratch_shapes=[
             pltpu.VMEM((LEVELS, 12, 2, 64, LON_LOCAL), bf16),
             pltpu.VMEM((LEVELS, ROWS, LON_LOCAL), bf16),
@@ -414,21 +450,22 @@
             pltpu.VMEM((256, 128), f32),
             pltpu.VMEM((2, 16, 64, 2, 512), bf16),
             pltpu.VMEM((STEPS, 4, Z_TOTAL, 32, 128), f32),
-            pltpu.VMEM((STEPS, 4, 4, 32, 128), f32),
+            pltpu.VMEM((STEPS, 4, X_TOTAL, 128), f32),
             pltpu.VMEM((STEPS, 2, Z_TOTAL // 2, 32, 128), f32),
             pltpu.VMEM((STEPS, 2, Z_TOTAL, 32, 128), f32),
             pltpu.VMEM((STEPS, 4, 3, 32, 128), f32),
-            pltpu.VMEM((STEPS, 2, 2, 32, 128), f32),
-            pltpu.VMEM((STEPS, 2, 4, 32, 128), f32),
-            pltpu.VMEM((STEPS, 3, 32, 128), f32),
+            pltpu.VMEM((STEPS, 2, X_HALF, 128), f32),
+            pltpu.VMEM((STEPS, 2, X_TOTAL, 128), f32),
+            pltpu.VMEM((STEPS, 4, 32, 128), f32),
+            pltpu.VMEM((CHUNKS, LEVELS, 16, WAVES), f32),
             dma((LEVELS,)),
+            dma((STEPS,)),
             dma((CHUNKS,)),
             dma((2,)),
             dma((STEPS,)),
             dma((STEPS,)),
             *[dma((STEPS, 2)) for _ in range(12)],
-            *[dma((STEPS, 4)) for _ in range(2)],
-            *[dma((STEPS, 3)) for _ in range(2)],
+            *[dma((STEPS, 4)) for _ in range(4)],
         ],
         compiler_params=pltpu.CompilerParams(
             collective_id=0, has_side_effects=True, vmem_limit_bytes=62 * 2**20

time: 109 us -> 108 us (level)
  no operation moved by 1% of the time
where the time goes in v4:
time: 108 us
  Pallas kernels  105 us (97%)
  local copies, waits for them, and re-layouts  3.01 us (3%)
    pallas_call x1, Pallas kernels, local(): pl.pallas_call(kernel, out_shape=jax.ShapeDtypeStruct((CHUNKS, LEVELS, 16...  105 us
    reshape x1, local copies, waits for them, and re-layouts, local(): spectral = result.reshape(1, CHUNKS, LEVELS, 2, 8, 2, WAVES // 2)  3.01 us

profile of v4, /device:TPU:0, one launch (start us, length us, event | category | flops | bytes accessed | tf_op | source)
XLA Modules:
  0.0 108.2 jit_solution(5517095380566486870)
XLA Ops:
  0.0 105.2 %spectral.1 = f32[8,2,16,1024]{3,2,1,0:T(8,128)} custom-call(bf16[12,2,2,64,512]{4,3,2,1,0:T(8,128)(2,1)} %grid_ref.1, f32[8,8,2,16,512]{4,3,2,1,0:T(8,128)} %constant.2.clone.table_ref, bf16[16,8,64,2,512]{4,3,2,1,0:T(2,128)(2,1)} %bitcast.5), custom_call_target="tpu_custom_call" | custom-call | tf_op jit(solution)/shard_map/spectral/pallas_call | solution.py:434
  105.2 3.0 %copy.6 = f32[1,8,2,2,8,2,512]{6,5,3,2,4,1,0:T(2,128)} copy(f32[1,8,2,2,8,2,512]{6,4,5,3,2,1,0:T(8,128)} %bitcast.6) | data formatting | bytes 2097152 | tf_op jit(solution)/shard_map/reshape | solution.py:475

commit v5 on v4

--- a/solution.py
+++ b/solution.py
@@ -95,6 +95,9 @@
             src_ref=src, dst_ref=dst, send_sem=s, recv_sem=q, device_id=dev, device_id_type=pl.DeviceIdType.MESH
         )
 
+    def arrived(ref, sem):
+        pltpu.make_async_copy(ref, ref, sem).wait()
+
     def table_copy(t):
         return pltpu.make_async_copy(table_ref.at[t], table.at[t], table_sem.at[t])
 
@@ -104,7 +107,7 @@
 
     def out_copy(t):
         at = (lax.rem(t, CHUNKS), t // CHUNKS)
-        return pltpu.make_async_copy(result.at[at], out_ref.at[at], out_sem.at[t])
+        return pltpu.make_async_copy(result.at[at], out_ref.at[at], out_sem)
 
     def grid_copy(level):
         return pltpu.make_async_copy(grid_ref.at[:, level], grid.at[level], grid_sem.at[level])
@@ -116,52 +119,52 @@
 
     def y1_copies(t):
         return (
-            send(paired.at[t, y_far, 0], y1_in.at[t, 0], y1_s.at[t, 0], y1_r.at[t, 0], lon_dev(y_up, core)),
-            send(paired.at[t, y_far, 1], y1_in.at[t, 1], y1_s.at[t, 1], y1_r.at[t, 1], lon_dev(y_down, core)),
+            send(paired.at[t, y_far, 0], y1_in.at[t, 0], y1_s.at[0], y1_r.at[t], lon_dev(y_up, core)),
+            send(paired.at[t, y_far, 1], y1_in.at[t, 1], y1_s.at[1], y1_r.at[t], lon_dev(y_down, core)),
         )
 
     def y2_copies(t):
         return (
-            send(paired.at[t, y_up], y2_in.at[t, 0], y2_s.at[t, 0], y2_r.at[t, 0], lon_dev(y_up, core)),
-            send(paired.at[t, y_down], y2_in.at[t, 1], y2_s.at[t, 1], y2_r.at[t, 1], lon_dev(y_down, core)),
+            send(paired.at[t, y_up], y2_in.at[t, 0], y2_s.at[0], y2_r.at[t], lon_dev(y_up, core)),
+            send(paired.at[t, y_down], y2_in.at[t, 1], y2_s.at[1], y2_r.at[t], lon_dev(y_down, core)),
         )
 
     z_half = Z_TOTAL // 2
 
     def z1_copies(t):
         return (
-            send(spec_z.at[t, z_far, 0:z_half], z1_in.at[t, 0], z1_s.at[t, 0], z1_r.at[t, 0], lat_dev(x, z_up)),
-            send(spec_z.at[t, z_far, z_half:Z_TOTAL], z1_in.at[t, 1], z1_s.at[t, 1], z1_r.at[t, 1], lat_dev(x, z_down)),
+            send(spec_z.at[t, z_far, 0:z_half], z1_in.at[t, 0], z1_s.at[0], z1_r.at[t], lat_dev(x, z_up)),
+            send(spec_z.at[t, z_far, z_half:Z_TOTAL], z1_in.at[t, 1], z1_s.at[1], z1_r.at[t], lat_dev(x, z_down)),
         )
 
     def z2_copies(t):
         return (
-            send(spec_z.at[t, z_up], z2_in.at[t, 0], z2_s.at[t, 0], z2_r.at[t, 0], lat_dev(x, z_up)),
-            send(spec_z.at[t, z_down], z2_in.at[t, 1], z2_s.at[t, 1], z2_r.at[t, 1], lat_dev(x, z_down)),
+            send(spec_z.at[t, z_up], z2_in.at[t, 0], z2_s.at[0], z2_r.at[t], lat_dev(x, z_up)),
+            send(spec_z.at[t, z_down], z2_in.at[t, 1], z2_s.at[1], z2_r.at[t], lat_dev(x, z_down)),
         )
 
     def x1_copies(t):
         return (
-            send(spec_x.at[t, x_far, 0:X_HALF], x1_in.at[t, 0], x1_s.at[t, 0], x1_r.at[t, 0], lat_dev(x_up, z)),
-            send(spec_x.at[t, x_far, X_HALF:X_TOTAL], x1_in.at[t, 1], x1_s.at[t, 1], x1_r.at[t, 1], lat_dev(x_down, z)),
+            send(spec_x.at[t, x_far, 0:X_HALF], x1_in.at[t, 0], x1_s.at[0], x1_r.at[t], lat_dev(x_up, z)),
+            send(spec_x.at[t, x_far, X_HALF:X_TOTAL], x1_in.at[t, 1], x1_s.at[1], x1_r.at[t], lat_dev(x_down, z)),
         )
 
     def x2_copies(t):
         return (
-            send(spec_x.at[t, x_up], x2_in.at[t, 0], x2_s.at[t, 0], x2_r.at[t, 0], lat_dev(x_up, z)),
-            send(spec_x.at[t, x_down], x2_in.at[t, 1], x2_s.at[t, 1], x2_r.at[t, 1], lat_dev(x_down, z)),
+            send(spec_x.at[t, x_up], x2_in.at[t, 0], x2_s.at[0], x2_r.at[t], lat_dev(x_up, z)),
+            send(spec_x.at[t, x_down], x2_in.at[t, 1], x2_s.at[1], x2_r.at[t], lat_dev(x_down, z)),
         )
 
     def zx_copy(t, source, to):
         n, first = Z_UNITS[to], Z_OFFSETS[to]
         return send(
-            spec_z.at[t, z, first : first + n], zx_in.at[t, source, 0:n], zx_s.at[t, to], zx_r.at[t, source], lat_dev(to, z)
+            spec_z.at[t, z, first : first + n], zx_in.at[t, source, 0:n], zx_s.at[to], zx_r.at[t], lat_dev(to, z)
         )
 
     def xz_copy(t, source, to):
         n, first = X_ROWS[to], X_OFFSETS[to]
         return send(
-            spec_x.at[t, x, first : first + n], xz_in.at[t, source, 0:n], xz_s.at[t, to], xz_r.at[t, source], lat_dev(x, to)
+            spec_x.at[t, x, first : first + n], xz_in.at[t, source, 0:n], xz_s.at[to], xz_r.at[t], lat_dev(x, to)
         )
 
     table_copy(0).start()
@@ -259,8 +262,7 @@
             copy.start()
 
     def y_forward(t):
-        for copy in y1_copies(t):
-            copy.wait_recv()
+        arrived(y1_in.at[t], y1_r.at[t])
         paired[t, y_up, 0] = paired[t, y_up, 0] + y1_in[t, 0]
         paired[t, y_down, 1] = paired[t, y_down, 1] + y1_in[t, 1]
         for copy in y2_copies(t):
@@ -268,8 +270,7 @@
 
     def project(t):
         slot = lax.rem(t, 2)
-        for copy in y2_copies(t):
-            copy.wait_recv()
+        arrived(y2_in.at[t], y2_r.at[t])
         for c in range(2):
             for f in range(8):
                 lanes = pl.ds(f * 128, 128)
@@ -302,22 +303,19 @@
             leg_copy(t + 2).start()
 
     def forward(t):
-        for copy in z1_copies(t):
-            copy.wait_recv()
+        arrived(z1_in.at[t], z1_r.at[t])
         spec_z[t, z_up, 0:z_half] = spec_z[t, z_up, 0:z_half] + z1_in[t, 0]
         spec_z[t, z_down, z_half:Z_TOTAL] = spec_z[t, z_down, z_half:Z_TOTAL] + z1_in[t, 1]
         for copy in z2_copies(t):
             copy.start()
-        for copy in x1_copies(t):
-            copy.wait_recv()
+        arrived(x1_in.at[t], x1_r.at[t])
         spec_x[t, x_up, 0:X_HALF] = spec_x[t, x_up, 0:X_HALF] + x1_in[t, 0]
         spec_x[t, x_down, X_HALF:X_TOTAL] = spec_x[t, x_down, X_HALF:X_TOTAL] + x1_in[t, 1]
         for copy in x2_copies(t):
             copy.start()
 
     def cross(t):
-        for copy in z2_copies(t):
-            copy.wait_recv()
+        arrived(z2_in.at[t], z2_r.at[t])
         spec_z[t, z] = spec_z[t, z] + (z2_in[t, 0] + z2_in[t, 1])
         for to in range(3):
 
@@ -325,8 +323,7 @@
             def _():
                 zx_copy(t, x, to).start()
 
-        for copy in x2_copies(t):
-            copy.wait_recv()
+        arrived(x2_in.at[t], x2_r.at[t])
         spec_x[t, x] = spec_x[t, x] + (x2_in[t, 0] + x2_in[t, 1])
         for to in range(4):
 
@@ -350,8 +347,8 @@
             def _():
                 n, first = Z_UNITS[mine], Z_OFFSETS[mine]
                 others = [source for source in range(4) if source != mine]
-                for source in others if n else ():
-                    zx_copy(t, source, mine).wait_recv()
+                if n:
+                    arrived(zx_in.at[t, 0:3, 0:n], zx_r.at[t])
                 for e in range(2):
                     rows = pl.ds(e * 16, 16)
                     for unit in range(n):
@@ -368,8 +365,7 @@
             def _():
                 n, first = X_ROWS[mine], X_OFFSETS[mine]
                 others = [source for source in range(4) if source != mine]
-                for source in others:
-                    xz_copy(t, source, mine).wait_recv()
+                arrived(xz_in.at[t, 0:3, 0:n], xz_r.at[t])
                 value = spec_x[t, x, first : first + n, :]
                 for source in others:
                     value = value + xz_in[t, source, 0:n, :]
@@ -401,30 +397,25 @@
 
     lax.fori_loop(0, STEPS + 8, steps, 0)
 
-    def drain(t, carry):
-        @pl.when(t >= STEPS - 2)
-        def _():
-            core_copy(t).wait_send()
-
-        ring = (*y1_copies(t), *y2_copies(t), *z1_copies(t), *z2_copies(t), *x1_copies(t), *x2_copies(t))
-        for copy in ring:
-            copy.wait_send()
-        out_copy(t).wait()
-        for to in range(4):
-
-            @pl.when(z != to)
-            def _():
-                xz_copy(t, z, to).wait_send()
-
-        for to in range(3):
-
-            @pl.when(x != to)
-            def _():
-                zx_copy(t, x, to).wait_send()
-
-        return carry
-
-    lax.fori_loop(0, STEPS, drain, 0)
+    for t in range(STEPS - 2, STEPS):
+        core_copy(t).wait_send()
+    pairs = ((y1_in, y1_s), (y2_in, y2_s), (z1_in, z1_s), (z2_in, z2_s), (x1_in, x1_s), (x2_in, x2_s))
+    for buffer, sems in pairs:
+        for way in range(2):
+            arrived(buffer.at[:, way], sems.at[way])
+    for to in range(3):
+
+        @pl.when(x != to)
+        def _():
+            arrived(zx_in.at[:, 0, 0 : Z_UNITS[to]], zx_s.at[to])
+
+    for to in range(4):
+
+        @pl.when(z != to)
+        def _():
+            arrived(xz_in.at[:, 0, 0 : X_ROWS[to]], xz_s.at[to])
+
+    arrived(result, out_sem)
 
 
 def local(grid, legendre):
@@ -459,13 +450,13 @@
             pltpu.VMEM((STEPS, 4, 32, 128), f32),
             pltpu.VMEM((CHUNKS, LEVELS, 16, WAVES), f32),
             dma((LEVELS,)),
-            dma((STEPS,)),
+            dma,
             dma((CHUNKS,)),
             dma((2,)),
             dma((STEPS,)),
             dma((STEPS,)),
-            *[dma((STEPS, 2)) for _ in range(12)],
-            *[dma((STEPS, 4)) for _ in range(4)],
+            *[dma((count,)) for _ in range(6) for count in (2, STEPS)],
+            *[dma((count,)) for _ in range(2) for count in (4, STEPS)],
         ],
         compiler_params=pltpu.CompilerParams(
             collective_id=0, has_side_effects=True, vmem_limit_bytes=62 * 2**20

time: 108 us -> 104 us (0.963)
  Pallas kernels: 105 us -> 101 us
    pallas_call x1, Pallas kernels: 105 us -> 101 us  [local(): pl.pallas_call(kernel, out_shape=jax.ShapeDtypeStruct((CHUNKS, LEVELS, 16...]
where the time goes in v5:
time: 104 us
  Pallas kernels  101 us (97%)
  local copies, waits for them, and re-layouts  3.01 us (3%)
    pallas_call x1, Pallas kernels, local(): pl.pallas_call(kernel, out_shape=jax.ShapeDtypeStruct((CHUNKS, LEVELS, 16...  101 us
    reshape x1, local copies, waits for them, and re-layouts, local(): spectral = result.reshape(1, CHUNKS, LEVELS, 2, 8, 2, WAVES // 2)  3.01 us

profile of v5, /device:TPU:0, one launch (start us, length us, event | category | flops | bytes accessed | tf_op | source)
XLA Modules:
  0.0 103.7 jit_solution(6395001463101040740)
XLA Ops:
  0.0 100.7 %spectral.1 = f32[8,2,16,1024]{3,2,1,0:T(8,128)} custom-call(bf16[12,2,2,64,512]{4,3,2,1,0:T(8,128)(2,1)} %grid_ref.1, f32[8,8,2,16,512]{4,3,2,1,0:T(8,128)} %constant.2.clone.table_ref, bf16[16,8,64,2,512]{4,3,2,1,0:T(2,128)(2,1)} %bitcast.5), custom_call_target="tpu_custom_call" | custom-call | tf_op jit(solution)/shard_map/spectral/pallas_call | solution.py:425
  100.7 3.0 %copy.6 = f32[1,8,2,2,8,2,512]{6,5,3,2,4,1,0:T(2,128)} copy(f32[1,8,2,2,8,2,512]{6,4,5,3,2,1,0:T(8,128)} %bitcast.6) | data formatting | bytes 2097152 | tf_op jit(solution)/shard_map/reshape | solution.py:466

commit v6 on v5

--- a/solution.py
+++ b/solution.py
@@ -204,12 +204,8 @@
 
         lax.fori_loop(0, 4, rows16, 0)
 
-    def rotate(t):
-        i = lax.rem(t, CHUNKS)
-
-        @pl.when(t < CHUNKS)
-        def _():
-            table_copy(i).wait()
+    def rotate(i):
+        table_copy(i).wait()
 
         def block_of(block, carry):
             q = 2 * lax.rem(block, 4) + block // 4
@@ -218,8 +214,8 @@
             for part_index, value in enumerate((real * c + imag * s, imag * c - real * s)):
                 high, low = split_bf16(value)
                 at = pl.multiple_of(block * 32 + part_index * 16, 16)
-                phases[pl.ds(at, 16), :] = high
-                phases[pl.ds(at + 256, 16), :] = low
+                phases[i, pl.ds(at, 16), :] = high
+                phases[i, pl.ds(at + 256, 16), :] = low
             return carry
 
         lax.fori_loop(0, 8, block_of, 0)
@@ -230,7 +226,7 @@
     pl.semaphore_wait(barrier, len(neighbours))
 
     def analyse(t):
-        slot, level = lax.rem(t, 2), t // CHUNKS
+        slot, i, level = lax.rem(t, 2), lax.rem(t, CHUNKS), t // CHUNKS
 
         @pl.when(t >= 2)
         def _():
@@ -238,13 +234,13 @@
 
         for n in range(ROWS // 256):
             rows = pl.ds(n * 256, 256)
-            both = lax.dot_general(phases[...], t_hi[level, rows, :], NT, preferred_element_type=jnp.float32)
-            rest = lax.dot_general(phases[0:256, :], t_lo[level, rows, :], NT, preferred_element_type=jnp.float32)
+            both = lax.dot_general(phases[i], t_hi[level, rows, :], NT, preferred_element_type=jnp.float32)
+            rest = lax.dot_general(phases[i, 0:256, :], t_lo[level, rows, :], NT, preferred_element_type=jnp.float32)
             value = both[0:256] + (both[256:512] + rest)
             part[slot, :, :, :, :, rows] = value.reshape(2, 4, 2, 16, 256)
         core_copy(t).start()
 
-        @pl.when(t + 1 < STEPS)
+        @pl.when(t + 1 < CHUNKS)
         def _():
             rotate(t + 1)
 
@@ -383,9 +379,9 @@
         t = step - 4
         stage(y_forward, t)
         stage(project, t - 1)
+        stage(pair_sum, t + 2)
         stage(forward, t - 2)
         stage(cross, t - 3)
-        stage(pair_sum, t + 2)
         stage(finish, t - 4)
         stage(analyse, t + 4)
 
@@ -433,7 +429,7 @@
             pltpu.VMEM((LEVELS, ROWS, LON_LOCAL), bf16),
             pltpu.VMEM((32, 32, 128), f32),
             pltpu.VMEM((CHUNKS, 8, 2, 16, LON_LOCAL), f32),
-            pltpu.VMEM((512, LON_LOCAL), bf16),
+            pltpu.VMEM((CHUNKS, 512, LON_LOCAL), bf16),
             pltpu.VMEM((2, 2, 4, 2, 16, ROWS), f32),
             pltpu.VMEM((STEPS, 4, 2, 16, ROWS), f32),
             pltpu.VMEM((STEPS, 2, 16, ROWS), f32),

time: 104 us -> 103 us (level)
  no operation moved by 1% of the time
where the time goes in v6:
time: 103 us
  Pallas kernels  100 us (97%)
  local copies, waits for them, and re-layouts  3.01 us (3%)
    pallas_call x1, Pallas kernels, local(): pl.pallas_call(kernel, out_shape=jax.ShapeDtypeStruct((CHUNKS, LEVELS, 16...  100 us
    reshape x1, local copies, waits for them, and re-layouts, local(): spectral = result.reshape(1, CHUNKS, LEVELS, 2, 8, 2, WAVES // 2)  3.01 us

profile of v6, /device:TPU:0, one launch (start us, length us, event | category | flops | bytes accessed | tf_op | source)
XLA Modules:
  0.0 103.1 jit_solution(4549265694982069118)
XLA Ops:
  0.0 100.1 %spectral.1 = f32[8,2,16,1024]{3,2,1,0:T(8,128)} custom-call(bf16[12,2,2,64,512]{4,3,2,1,0:T(8,128)(2,1)} %grid_ref.1, f32[8,8,2,16,512]{4,3,2,1,0:T(8,128)} %constant.2.clone.table_ref, bf16[16,8,64,2,512]{4,3,2,1,0:T(2,128)(2,1)} %bitcast.5), custom_call_target="tpu_custom_call" | custom-call | tf_op jit(solution)/shard_map/spectral/pallas_call | solution.py:421
  100.1 3.0 %copy.6 = f32[1,8,2,2,8,2,512]{6,5,3,2,4,1,0:T(2,128)} copy(f32[1,8,2,2,8,2,512]{6,4,5,3,2,1,0:T(8,128)} %bitcast.6) | data formatting | bytes 2097152 | tf_op jit(solution)/shard_map/reshape | solution.py:462

commit v7 on v6

--- a/solution.py
+++ b/solution.py
@@ -385,7 +385,7 @@
         stage(finish, t - 4)
         stage(analyse, t + 4)
 
-        @pl.when(t == 0)
+        @pl.when(t == 3)
         def _():
             fields(1)
 

time: 103 us -> 104 us (level)
  no operation moved by 1% of the time
where the time goes in v7:
time: 104 us
  Pallas kernels  100 us (96%)
  local copies, waits for them, and re-layouts  3.01 us (3%)
    pallas_call x1, Pallas kernels, local(): pl.pallas_call(kernel, out_shape=jax.ShapeDtypeStruct((CHUNKS, LEVELS, 16...  100 us
    reshape x1, local copies, waits for them, and re-layouts, local(): spectral = result.reshape(1, CHUNKS, LEVELS, 2, 8, 2, WAVES // 2)  3.01 us

profile of v7, /device:TPU:0, one launch (start us, length us, event | category | flops | bytes accessed | tf_op | source)
XLA Modules:
  0.0 103.5 jit_solution(14172030759359927536)
XLA Ops:
  0.0 100.5 %spectral.1 = f32[8,2,16,1024]{3,2,1,0:T(8,128)} custom-call(bf16[12,2,2,64,512]{4,3,2,1,0:T(8,128)(2,1)} %grid_ref.1, f32[8,8,2,16,512]{4,3,2,1,0:T(8,128)} %constant.2.clone.table_ref, bf16[16,8,64,2,512]{4,3,2,1,0:T(2,128)(2,1)} %bitcast.5), custom_call_target="tpu_custom_call" | custom-call | tf_op jit(solution)/shard_map/spectral/pallas_call | solution.py:421
  100.5 3.0 %copy.6 = f32[1,8,2,2,8,2,512]{6,5,3,2,4,1,0:T(2,128)} copy(f32[1,8,2,2,8,2,512]{6,4,5,3,2,1,0:T(8,128)} %bitcast.6) | data formatting | bytes 2097152 | tf_op jit(solution)/shard_map/reshape | solution.py:462
